TPU v7x, 512 devices: a whole 4x8x8 slice. The times are simulated.
512 devices in a mesh: own: 128 (over y, z, core), rep: 4 (over x).
Axes of the slice: x: 4, y: 8, z: 8, core: 2. Of those that a mesh axis runs over, the one named last changes fastest.
Arguments:
- node_rows: bfloat16 [65536, 256], P(('own', 'rep')), may hold values from -6 to 6
- w_query: bfloat16 [256, 256], replicated, may hold values from -0.375 to 0.375
- w_keyval: bfloat16 [256, 512], replicated, may hold values from -0.375 to 0.375
- need_rows: int32 [128, 128, 4, 1], P(None, 'own'), may hold values from 0 to 127
- neighbours: int32 [65536, 16], P(('own', 'rep')), may hold values from 0 to 1023, as said below
- grad_out: bfloat16 [65536, 256], P(('own', 'rep')), may hold values from -6 to 6
Outputs:
- attended: bfloat16 [65536, 256], P(('own', 'rep'))
- grad_nodes: bfloat16 [65536, 256], P(('own', 'rep'))
- grad_query: float32 [256, 256], replicated
- grad_keyval: float32 [256, 512], replicated
Inputs may be any that keep to these rules, and one draw needn't show every extreme that they name: `neighbours`: the first 2 entries of each node's list together name every received row of its group's table; the rest are spread over the whole table.
All inputs are finite; a program needn't handle non-finite values.
Results may differ from a plain program's by a relative error of at most 0.02.
Values may be sent and summed in bfloat16 or wider, within the bound.
No kernel may reach another device: no remote copies, remote signals or barrier semaphores. Data moves between devices by JAX's collectives and lax.ppermute only.
A program may use at most 64 MiB of HBM per device.

v0:
```python
import math

import jax
import jax.numpy as jnp
from jax import lax
from jax.sharding import PartitionSpec as P

HEADS = 4
HEAD_DIM = 64


def shards(node_rows, w_query, w_keyval, need_rows, neighbours, grad_out):
    local_rows, features = node_rows.shape
    owners = lax.axis_size("own")
    replicas = lax.axis_size("rep")
    degree = neighbours.shape[1]
    slot_count = need_rows.shape[3]
    group_size = replicas * local_rows
    score_scale = 1.0 / math.sqrt(HEAD_DIM)
    wanted = need_rows[:, 0]
    my_rows = lax.dynamic_index_in_dim(wanted, lax.axis_index("rep"), 1, keepdims=False)
    outgoing = jnp.take(node_rows, my_rows.reshape(-1), axis=0).reshape(
        owners, slot_count, features
    )
    incoming = lax.all_to_all(outgoing, "own", split_axis=0, concat_axis=0, tiled=True)
    group_block, arrived = (
        lax.all_gather(node_rows, "rep", axis=0, tiled=True),
        lax.all_gather(incoming, "rep", axis=0, tiled=True),
    )
    arrived = arrived.reshape(-1, features)
    sources = jnp.concatenate([group_block, arrived], 0)
    table_rows = sources.shape[0]
    queries = jnp.dot(node_rows, w_query, preferred_element_type=jnp.float32).astype(jnp.bfloat16)
    keyval = jnp.dot(sources, w_keyval, preferred_element_type=jnp.float32).astype(jnp.bfloat16)
    gathered = jnp.take(keyval, neighbours.reshape(-1), axis=0).reshape(
        local_rows, degree, 2 * features
    )
    key_rows = gathered[:, :, :features].reshape(local_rows, degree, HEADS, HEAD_DIM)
    value_rows = gathered[:, :, features:].reshape(local_rows, degree, HEADS, HEAD_DIM)
    query_heads = queries.reshape(local_rows, HEADS, HEAD_DIM)
    scores = (
        jnp.einsum("ghd,gjhd->gjh", query_heads, key_rows, preferred_element_type=jnp.float32)
        * score_scale
    )
    weights = jnp.exp(scores)
    attention = weights / jnp.sum(weights, axis=1, keepdims=True)
    attention_b = attention.astype(jnp.bfloat16)
    attended = (
        jnp.einsum("gjh,gjhd->ghd", attention_b, value_rows, preferred_element_type=jnp.float32)
        .astype(jnp.bfloat16)
        .reshape(local_rows, features)
    )
    upstream = grad_out.reshape(local_rows, HEADS, HEAD_DIM)
    dprob = jnp.einsum("ghd,gjhd->gjh", upstream, value_rows, preferred_element_type=jnp.float32)
    dscore = (
        attention * (dprob - jnp.sum(attention * dprob, axis=1, keepdims=True)) * score_scale
    ).astype(jnp.bfloat16)
    dquery = (
        jnp.einsum("gjh,gjhd->ghd", dscore, key_rows, preferred_element_type=jnp.float32)
        .astype(jnp.bfloat16)
        .reshape(local_rows, features)
    )
    edge_ids = neighbours.reshape(-1)
    contrib_key = (
        dscore.astype(jnp.float32)[..., None] * query_heads.astype(jnp.float32)[:, None]
    ).reshape(local_rows * degree, features)
    contrib_value = (
        attention_b.astype(jnp.float32)[..., None] * upstream.astype(jnp.float32)[:, None]
    ).reshape(local_rows * degree, features)
    contrib = jnp.concatenate([contrib_key, contrib_value], 1)
    partial_kv = jax.ops.segment_sum(contrib, edge_ids, num_segments=table_rows).astype(
        jnp.bfloat16
    )
    partial_src = jnp.dot(partial_kv, w_keyval.T, preferred_element_type=jnp.float32)
    own_sum, arrived_sum = (
        lax.psum_scatter(
            partial_src[:group_size].astype(jnp.bfloat16), "rep", scatter_dimension=0, tiled=True
        ).astype(jnp.float32),
        lax.psum_scatter(
            partial_src[group_size:].astype(jnp.bfloat16), "rep", scatter_dimension=0, tiled=True
        ).astype(jnp.float32),
    )
    sent_back = lax.all_to_all(
        arrived_sum.reshape(owners, slot_count, features).astype(jnp.bfloat16),
        "own",
        split_axis=0,
        concat_axis=0,
        tiled=True,
    ).astype(jnp.float32)
    returned = jax.ops.segment_sum(
        sent_back.reshape(-1, features), my_rows.reshape(-1), num_segments=local_rows
    )
    node_part = own_sum + returned
    grad_q = jnp.dot(node_rows.T, dquery, preferred_element_type=jnp.float32)
    grad_kv = jnp.dot(sources.T, partial_kv, preferred_element_type=jnp.float32)
    grad_q, grad_kv = lax.psum((grad_q, grad_kv), ("own", "rep"))
    grad_nodes = (
        node_part + jnp.dot(dquery, w_query.T, preferred_element_type=jnp.float32)
    ).astype(jnp.bfloat16)
    return (attended, grad_nodes, grad_q, grad_kv)


def solution(mesh):
    in_specs = (
        P(("own", "rep"), None),
        P(),
        P(),
        P(None, "own", None, None),
        P(("own", "rep"), None),
        P(("own", "rep"), None),
    )
    out_specs = (P(("own", "rep"), None), P(("own", "rep"), None), P(), P())
    return jax.shard_map(shards, mesh=mesh, in_specs=in_specs, out_specs=out_specs, check_vma=False)
```

profile of v0, /device:TPU:1, one launch (start us, length us, event | category | flops | bytes accessed | tf_op | source)
XLA Modules:
  0.0 431.4 jit_solution(8424495473816167622)
XLA Ops:
  8.0 0.7 fusion.22
  8.8 0.7 compare_and_fusion.1
  9.4 1.6 gather_fusion
  11.1 0.5 broadcast.114
  11.6 0.6 reduce.8
  12.2 0.7 reshape.228
  12.8 18.4 %all-to-all-start = ((bf16[128,2,128]{2,1,0:T(2,128)(2,1)}), bf16[128,2,128]{2,1,0:T(2,128)(2,1)S(1)}, u32[]{:S(2)}, u32[]{:S(2)}) async-start(bf16[128,2,128]{2,1,0:T(2,128)(2,1)} %reshape.228), calls=%async_computation | async-start | bytes 131072 | tf_op jit(solution)/shard_map/all_to_all | solution.py:25
  31.3 1.0 copy.41
  32.3 1.1 convolution_convert_fusion.2
  33.5 0.8 copy.37
  34.6 0.8 copy.43
  35.4 0.8 copy.42
  36.3 10.9 %all_gather.6 = bf16[512,256]{1,0:T(8,128)(2,1)S(1)} all-gather(bf16[128,256]{1,0:T(8,128)(2,1)S(1)} %copy-done.1), channel_id=1, replica_groups=mesh['own'=128,'rep'=4] {'rep'}, dimensions={0}, use_global_device_ids=true | all-gather | bytes 327680 | tf_op jit(solution)/shard_map/all_gather | solution.py:27
  47.2 9.4 %all_gather.7 = bf16[512,1,256]{2,0,1:T(8,128)(2,1)S(1)} all-gather(bf16[128,1,256]{2,0,1:T(8,128)(2,1)S(1)} %copy.36), channel_id=1, replica_groups=mesh['own'=128,'rep'=4] {'rep'}, dimensions={0}, use_global_device_ids=true | all-gather | bytes 327680 | tf_op jit(solution)/shard_map/all_gather | solution.py:28
  56.6 0.7 copy-done.4
  57.3 0.4 convolution_convert_fusion
  57.7 7.7 %gather_fusion.1 = bf16[2048,512]{1,0:T(8,128)(2,1)S(1)} fusion(bf16[1024,512]{1,0:T(8,128)(2,1)S(1)} %convolution_convert_fusion, s32[2048]{0:T(1024)S(1)} %broadcast_clamp_fusion), kind=kCustom, calls=%fused_computation.1 | custom fusion | bytes 4202496 | tf_op jit(solution)/shard_map/jit(_take)/gather | solution.py:35
  65.5 3.1 copy.38
  68.6 1.8 broadcast_select_fusion
  70.5 1.2 multiply_reduce_fusion.3
  71.6 0.5 copy.54
  72.1 2.1 convert_convert_fusion
  74.2 0.5 copy.68
  74.8 3.2 fusion.29
  78.0 2.2 copy.79
  80.2 5.2 %broadcast_multiply_fusion = f32[128,16,4,64]{3,2,1,0:T(4,128)} fusion(f32[128,4,64]{2,1,0:T(4,128)} %copy.43, f32[128,16,4]{2,1,0:T(8,128)} %get-tuple-element.30), kind=kLoop, calls=%fused_computation.14 | loop fusion | flops 524288 | bytes 2260992 | tf_op jit(solution)/shard_map/mul | solution.py:68
  85.4 5.4 %mul.58 = f32[2048,256]{1,0:T(8,128)} reshape(f32[128,16,4,64]{3,2,1,0:T(4,128)} %broadcast_multiply_fusion) | data formatting | bytes 4194304 | tf_op jit(solution)/shard_map/mul | solution.py:68
  90.8 4.9 %broadcast_multiply_fusion.1 = f32[128,16,4,64]{3,2,1,0:T(4,128)} fusion(f32[128,4,64]{2,1,0:T(4,128)} %copy.42, f32[128,16,4]{2,1,0:T(8,128)S(1)} %copy-done.2), kind=kLoop, calls=%fused_computation.15 | loop fusion | flops 524288 | bytes 2260992 | tf_op jit(solution)/shard_map/mul | solution.py:65
  95.6 5.3 %mul.54 = f32[2048,256]{1,0:T(8,128)} reshape(f32[128,16,4,64]{3,2,1,0:T(4,128)} %broadcast_multiply_fusion.1) | data formatting | bytes 4194304 | tf_op jit(solution)/shard_map/mul | solution.py:65
  101.2 0.9 convolution_bitcast_fusion
  102.1 14.2 %scatter_custom_fusion = f32[1024,512]{1,0:T(8,128)S(1)} fusion(s32[2048]{0:T(1024)S(1)} %reshape.200, f32[2048,256]{1,0:T(8,128)} %mul.58, f32[]{:T(128)} %constant.54, f32[2048,256]{1,0:T(8,128)} %mul.54, f32[]{:T(128)} %constant.45.clone.1), kind=kCustom, calls=%fused_computation.6 | custom fusion | flops 2097152 | bytes 6291464 | tf_op jit(solution)/shard_map/scatter-add | solution.py:71
  116.3 2.3 fusion.14
  118.7 0.5 convolution_convert_fusion.1
  119.2 0.9 fusion.28
  120.1 0.5 reduce-scatter.3.cloned.1.call-update
  120.6 0.4 copy.77
  121.1 0.3 multiply_reduce_fusion.2
  121.4 0.7 copy.46
  122.1 274.1 %all-reduce.3.cloned.1.call-done = (f32[256,256]{0,1:T(8,128)}, f32[256,512]{1,0:T(8,128)}) async-done(((f32[256,256]{0,1:T(8,128)}, f32[256,512]{1,0:T(8,128)}), (f32[256,256]{0,1:T(8,128)}, f32[256,512]{1,0:T(8,128)})) %all-reduce.3.cloned.1.call-update) | async-done | bytes 786448 | tf_op jit(solution)/shard_map/psum | solution.py:96
  396.2 1.8 copy.47
  398.0 1.4 reduce.9
  399.4 0.7 reshape.230
  400.1 9.6 %all-to-all-start.1 = ((bf16[128,2,128]{2,1,0:T(2,128)(2,1)}), bf16[128,2,128]{2,1,0:T(2,128)(2,1)S(1)}, u32[]{:S(2)}, u32[]{:S(2)}) async-start(bf16[128,2,128]{2,1,0:T(2,128)(2,1)} %reshape.230), calls=%async_computation.3 | async-start | bytes 131072 | tf_op jit(solution)/shard_map/all_to_all | solution.py:83
  409.7 1.0 convolution_add_fusion
  410.8 10.4 %all-to-all-done.1 = bf16[128,2,128]{2,1,0:T(2,128)(2,1)S(1)} async-done(((bf16[128,2,128]{2,1,0:T(2,128)(2,1)}), bf16[128,2,128]{2,1,0:T(2,128)(2,1)S(1)}, u32[]{:S(2)}, u32[]{:S(2)}) %all-to-all-start.1) | async-done | bytes 65568 | tf_op jit(solution)/shard_map/all_to_all | solution.py:83
  421.2 1.4 scatter_custom_fusion.1
  422.6 0.6 convert_element_type.68
  423.2 0.8 copy.91
  (48 shorter events, 1.0 us)
Async XLA Ops:
  8.0 49.3 %copy-start = (bf16[256,512]{1,0:T(8,128)(2,1)S(1)}, bf16[256,512]{1,0:T(8,128)(2,1)}, u32[]{:S(2)}) copy-start(bf16[256,512]{1,0:T(8,128)(2,1)} %param.8) | copy-start | bytes 786436
  8.0 28.2 %copy-start.1 = (bf16[128,256]{1,0:T(8,128)(2,1)S(1)}, bf16[128,256]{1,0:T(8,128)(2,1)}, u32[]{:S(2)}) copy-start(bf16[128,256]{1,0:T(8,128)(2,1)} %param.6) | copy-start | bytes 196612
  8.0 26.4 %copy-start.13 = (s32[128,16]{0,1:T(8,128)S(1)}, s32[128,16]{0,1:T(8,128)}, u32[]{:S(2)}) copy-start(s32[128,16]{0,1:T(8,128)} %param.10) | copy-start | bytes 24580
  12.8 34.3 %all-to-all-start = ((bf16[128,2,128]{2,1,0:T(2,128)(2,1)}), bf16[128,2,128]{2,1,0:T(2,128)(2,1)S(1)}, u32[]{:S(2)}, u32[]{:S(2)}) async-start(bf16[128,2,128]{2,1,0:T(2,128)(2,1)} %reshape.228), calls=%async_computation | async-start | bytes 131072 | tf_op jit(solution)/shard_map/all_to_all | solution.py:25
  31.3 364.9 %all-reduce.3.cloned.1.call-start = ((), (), s32[]{:S(2)}) async-start(), calls=%async_computation.6 | async-start | bytes 1572864 | tf_op jit(solution)/shard_map/psum | solution.py:96
  34.5 22.1 %copy-start.5 = (f32[128,4,64]{0,2,1:T(8,128)}, f32[128,4,64]{0,2,1:T(8,128)S(1)}, u32[]{:S(2)}) copy-start(f32[128,4,64]{0,2,1:T(8,128)S(1)} %get-tuple-element.37) | copy-start | bytes 393220
  34.5 22.1 %copy-start.7 = (f32[128,4,64]{0,2,1:T(8,128)}, f32[128,4,64]{0,2,1:T(8,128)S(1)}, u32[]{:S(2)}) copy-start(f32[128,4,64]{0,2,1:T(8,128)S(1)} %get-tuple-element.38) | copy-start | bytes 393220
  47.2 9.4 %copy-start.3 = (bf16[512,256]{1,0:T(8,128)(2,1)}, bf16[512,256]{1,0:T(8,128)(2,1)S(1)}, u32[]{:S(2)}) copy-start(bf16[512,256]{1,0:T(8,128)(2,1)S(1)} %all_gather.6) | copy-start | bytes 786436
  56.6 0.7 copy-start.4
  68.6 1.8 copy-start.6
  68.6 1.9 copy-start.8
  85.4 5.4 %copy-start.2 = (f32[128,16,4]{2,1,0:T(8,128)S(1)}, f32[128,16,4]{2,1,0:T(8,128)}, u32[]{:S(2)}) copy-start(f32[128,16,4]{2,1,0:T(8,128)} %get-tuple-element.34) | copy-start | bytes 98308
  95.6 5.3 %copy-start.12 = (f32[128,4,16]{0,1,2:T(4,128)S(1)}, f32[128,4,16]{0,1,2:T(4,128)}, u32[]{:S(2)}) copy-start(f32[128,4,16]{0,1,2:T(4,128)} %copy.79) | copy-start | bytes 98308
  118.6 279.4 %reduce-scatter.5.cloned.1.call-start = ((), (), s32[]{:S(2)}) async-start(), calls=%async_computation.5 | async-start | bytes 327680 | tf_op jit(solution)/shard_map/reduce_scatter | solution.py:79
  119.1 1.5 copy-start.9
  120.0 289.7 %copy-start.10 = (bf16[256,256]{1,0:T(8,128)(2,1)S(1)}, bf16[256,256]{1,0:T(8,128)(2,1)}, u32[]{:S(2)}) copy-start(bf16[256,256]{1,0:T(8,128)(2,1)} %param.7) | copy-start | bytes 393220
  120.0 289.7 %reduce-scatter.3.cloned.1.call-start = ((), (), s32[]{:S(2)}) async-start(), calls=%async_computation.4 | async-start | bytes 327680 | tf_op jit(solution)/shard_map/reduce_scatter | solution.py:76
  396.2 27.0 %copy-start.11 = (f32[256,512]{1,0:T(8,128)S(1)}, f32[256,512]{1,0:T(8,128)}, u32[]{:S(2)}) copy-start(f32[256,512]{1,0:T(8,128)} %get-tuple-element.42) | copy-start | bytes 1572868
  400.1 21.1 %all-to-all-start.1 = ((bf16[128,2,128]{2,1,0:T(2,128)(2,1)}), bf16[128,2,128]{2,1,0:T(2,128)(2,1)S(1)}, u32[]{:S(2)}, u32[]{:S(2)}) async-start(bf16[128,2,128]{2,1,0:T(2,128)(2,1)} %reshape.230), calls=%async_computation.3 | async-start | bytes 131072 | tf_op jit(solution)/shard_map/all_to_all | solution.py:83
Sparse Core Ops, SparseCore 0:
  118.7 277.4 all-reduce.2
Sparse Core Ops, SparseCore 1:
  121.9 29.3 reduce-scatter.4
  154.1 25.3 reduce-scatter.2
where the time goes:
time: 432 us; the launch traced here: 431 us
  waiting for transfers between devices  285 us (66%)
  other arithmetic  38.6 us (9%)
  local copies, waits for them, and re-layouts  37.4 us (9%)
  starting transfers between devices  28.2 us (7%)
  blocking collectives  20.3 us (5%)
  between operations  15.8 us (4%)
  matrix products  6.2 us (1%)
    psum x1, waiting for transfers between devices, shards(): grad_q, grad_kv = lax.psum((grad_q, grad_kv), ('own', 'rep'))  274 us
    all_to_all x1, starting transfers between devices, shards(): lax.all_to_all(outgoing, 'own', split_axis=0, concat_axis=0, tiled=True)  18.4 us
    scatter-add x1, other arithmetic, shards(): jax.ops.segment_sum(contrib, edge_ids, num_segments=table_rows)  14.2 us
    all_gather x1, blocking collectives, shards(): lax.all_gather(node_rows, 'rep', axis=0, tiled=True)  10.9 us
    gather x2, local copies, waits for them, and re-layouts, shards(): jnp.take(keyval, neighbours.reshape(-1), axis=0)  10.8 us
    all_to_all x1, waiting for transfers between devices, shards(): lax.all_to_all(arrived_sum.reshape(owners, slot_count, features).astype(j...  10.4 us
    unnamed x39, local copies, waits for them, and re-layouts  9.92 us
    all_to_all x1, starting transfers between devices, shards(): lax.all_to_all(arrived_sum.reshape(owners, slot_count, features).astype(j...  9.61 us
  transfers between devices with their start and end apart: 5, of which 2 were waited for; matrix products, arithmetic and copies ran while one was open for 3% of the time, Pallas kernels for 0%

commit v1 on v0

v1 whole, which is shorter than its diff:
```python
import math

import jax
import jax.numpy as jnp
from jax import lax
from jax.experimental import pallas as pl
from jax.experimental.pallas import tpu as pltpu
from jax.sharding import Mesh
from jax.sharding import PartitionSpec as P

HEADS = 4
HEAD_DIM = 64
LANES = 128
BF16, F32 = jnp.bfloat16, jnp.float32


def dot(a, b, contract=((1,), (0,))):
    return lax.dot_general(a, b, (contract, ((), ())), preferred_element_type=F32)


def rows_of_both(a, b):
    return dot(a, b, ((1,), (1,)))


def columns_of_both(a, b):
    return dot(a, b, ((0,), (0,)))


def exchange(blocks, axes):
    return lax.all_to_all(blocks, axes, split_axis=0, concat_axis=0, tiled=True)


def spread(block, axes, count):
    return exchange(jnp.broadcast_to(block[None], (count,) + block.shape), axes)


def per_head(rows):
    head = lax.broadcasted_iota(jnp.int32, rows.shape, 1) // HEAD_DIM
    wide = rows.astype(F32)
    return jnp.concatenate([jnp.where(head == h, wide, 0.0) for h in range(HEADS)], 0)


def own_blocks(table, nodes):
    blocks = [
        table[h * HEAD_DIM : (h + 1) * HEAD_DIM, h * nodes : (h + 1) * nodes] for h in range(HEADS)
    ]
    return jnp.concatenate(blocks, 0).T


def attention_kernel(
    node_ref, grad_ref, links_ref, table_ref, wq_ref, wkv_ref,
    attended_ref, send_ref, dnode_ref, weight_scr, dprob_scr,
):
    nodes, features = node_ref.shape
    degree = links_ref.shape[0]
    replicas = send_ref.shape[0]
    block = table_ref.shape[0] // replicas
    scale = 1.0 / math.sqrt(HEAD_DIM)
    node = node_ref[...]
    wkv = wkv_ref[...]
    queries = per_head(dot(node, wq_ref[...]).astype(BF16))
    upstream = per_head(grad_ref[...])
    q_heads, q_scaled = queries.astype(BF16), (queries * scale).astype(BF16)
    g_heads, g_scaled = upstream.astype(BF16), (upstream * scale).astype(BF16)

    links = links_ref[...]
    arrived = links >= replicas * nodes
    owner = jnp.where(arrived, links - replicas * nodes, links) // nodes
    links = owner * block + jnp.where(arrived, nodes, 0) + links % nodes

    keyval = []
    total = jnp.zeros((1, HEADS * nodes), F32)
    inner = jnp.zeros((1, HEADS * nodes), F32)
    for r in range(replicas):
        span = slice(r * block, (r + 1) * block)
        kv = dot(table_ref[span, :], wkv).astype(BF16)
        keyval.append(kv)
        here = lax.broadcasted_iota(jnp.int32, (block, nodes), 0) + r * block
        count = jnp.zeros((block, nodes), F32)
        for j in range(degree):
            count = count + jnp.where(here == links[j : j + 1, :], 1.0, 0.0)
        log_count = jnp.where(count > 0.0, jnp.log(jnp.maximum(count, 1.0)), -1e30)
        log_count = jnp.concatenate([log_count] * HEADS, 1)
        weight = jnp.exp(rows_of_both(kv[:, :features], q_scaled) + log_count)
        dprob = rows_of_both(kv[:, features:], g_scaled)
        total = total + jnp.sum(weight, axis=0, keepdims=True)
        inner = inner + jnp.sum(weight * dprob, axis=0, keepdims=True)
        weight_scr[span, :] = weight
        dprob_scr[span, :] = dprob

    inverse = 1.0 / total
    mean = inner * inverse
    attended = jnp.zeros((features, HEADS * nodes), F32)
    dquery = jnp.zeros((features, HEADS * nodes), F32)
    grad_kv = jnp.zeros(wkv.shape, F32)
    for r in range(replicas):
        span = slice(r * block, (r + 1) * block)
        kv = keyval[r]
        prob = weight_scr[span, :] * inverse
        dscore = (prob * (dprob_scr[span, :] - mean)).astype(BF16)
        prob = prob.astype(BF16)
        attended = attended + columns_of_both(kv[:, features:], prob)
        dquery = dquery + columns_of_both(kv[:, :features], dscore)
        dkv = jnp.concatenate([dot(dscore, q_heads), dot(prob, g_heads)], 1).astype(BF16)
        grad_kv = grad_kv + columns_of_both(table_ref[span, :], dkv)
        dsrc = rows_of_both(dkv, wkv).astype(BF16)
        for part in range(2):
            for half in range(2):
                at = (part * 2 + half) * nodes
                send_ref[r, at : at + nodes, :] = dsrc[
                    part * nodes : (part + 1) * nodes, half * LANES : (half + 1) * LANES
                ]

    attended_ref[...] = own_blocks(attended, nodes).astype(BF16)
    dquery = own_blocks(dquery, nodes).astype(BF16)
    dnode_ref[...] = rows_of_both(dquery, wq_ref[...])
    grads = jnp.concatenate([columns_of_both(node, dquery), grad_kv], 1).astype(BF16)
    pieces = features * grads.shape[1] // (LANES * LANES)
    each = pieces // replicas
    down = features // LANES
    for piece in range(pieces):
        column, row = (piece // down) * LANES, (piece % down) * LANES
        at = 4 * nodes + (piece % each) * LANES
        send_ref[piece // each, at : at + LANES, :] = grads[row : row + LANES, column : column + LANES]


def attention(node_rows, grad_out, links, table, w_query, w_keyval, replicas):
    nodes, features = node_rows.shape
    entries = table.shape[0]
    sent = 4 * nodes + features * (features + w_keyval.shape[1]) // LANES // replicas
    whole = pl.BlockSpec(memory_space=pltpu.VMEM)
    return pl.pallas_call(
        attention_kernel,
        out_shape=(
            jax.ShapeDtypeStruct((nodes, features), BF16),
            jax.ShapeDtypeStruct((replicas, sent, LANES), BF16),
            jax.ShapeDtypeStruct((nodes, features), F32),
        ),
        in_specs=[whole] * 6,
        out_specs=(whole,) * 3,
        scratch_shapes=[pltpu.VMEM((entries, HEADS * nodes), F32)] * 2,
        compiler_params=pltpu.CompilerParams(vmem_limit_bytes=48 * 1024 * 1024),
        name="attention",
    )(node_rows, grad_out, links, table, w_query, w_keyval)


def shards(node_rows, w_query, w_keyval, need_rows, neighbours, grad_out):
    nodes, features = node_rows.shape
    ny, nz, nc, replicas = (lax.axis_size(a) for a in ("y", "z", "c", "x"))
    inner = nz * nc
    owners = ny * inner

    wanted = need_rows.reshape(owners, replicas).T
    my_rows = lax.dynamic_index_in_dim(wanted, lax.axis_index("x"), 0, keepdims=False)
    picks = (my_rows[:, None] == jnp.arange(nodes, dtype=jnp.int32)[None, :]).astype(BF16)
    outgoing = dot(picks, node_rows).astype(BF16)
    incoming = exchange(outgoing, ("y", "z", "c"))
    table = spread(jnp.concatenate([node_rows, incoming], 0), "x", replicas)
    table = table.reshape(-1, features)

    attended, partial, dnode = attention(
        node_rows, grad_out, neighbours.T, table, w_query, w_keyval, replicas
    )

    summed = jnp.sum(exchange(partial, "x").astype(F32), 0)
    own = jnp.concatenate([summed[:nodes], summed[nodes : 2 * nodes]], 1)
    back = summed[2 * nodes : 4 * nodes].astype(BF16).reshape(2, ny, inner, LANES)
    grads = summed[4 * nodes :].astype(BF16).reshape(inner, -1, LANES)
    kept = grads.shape[1]
    back = back.transpose(2, 0, 1, 3).reshape(inner, 2 * ny, LANES)
    landed = exchange(jnp.concatenate([back, grads], 1), ("z", "c"))
    back = landed[:, : 2 * ny].reshape(inner, 2, ny, LANES).transpose(2, 1, 0, 3)
    back = back.reshape(ny, 2 * inner, LANES)
    grads = jnp.sum(landed[:, 2 * ny :].astype(F32), 0).astype(BF16)
    grads = jnp.broadcast_to(grads[None], (ny, kept, LANES))
    landed = exchange(jnp.concatenate([back, grads], 1), "y")
    returned = jnp.concatenate(
        [
            landed[:, :inner].reshape(owners, LANES),
            landed[:, inner : 2 * inner].reshape(owners, LANES),
        ],
        1,
    )
    grad_nodes = (own + dnode + columns_of_both(picks, returned)).astype(BF16)
    grads = jnp.sum(landed[:, 2 * inner :].astype(F32), 0).astype(BF16)
    grads = spread(grads, ("z", "c"), inner).reshape(-1, LANES)
    grads = spread(grads, "x", replicas).reshape(-1, features, LANES).astype(F32)
    grads = grads.transpose(1, 0, 2).reshape(features, -1)
    return attended, grad_nodes, grads[:, :features], grads[:, features:]


def solution(mesh):
    own, rep = mesh.devices.shape
    side = math.isqrt(own // 2)
    fine = Mesh(mesh.devices.reshape(side, own // 2 // side, 2, rep), ("y", "z", "c", "x"))
    rows = P(("y", "z", "c", "x"), None)
    in_specs = (rows, P(), P(), P(None, ("y", "z", "c"), None, None), rows, rows)
    return jax.shard_map(
        shards, mesh=fine, in_specs=in_specs, out_specs=(rows, rows, P(), P()), check_vma=False
    )
```

time: 432 us -> 121 us (0.28)
  waiting for transfers between devices: 285 us -> 15.8 us
  blocking collectives: 20.3 us -> 83.2 us
  other arithmetic: 38.6 us -> 0.94 us
  local copies, waits for them, and re-layouts: 37.4 us -> 5 us
  starting transfers between devices: 28.2 us -> 7.18 us
  between operations: 15.8 us -> 0.87 us
  Pallas kernels: 0 us -> 5.04 us
    psum x1 -> x0, waiting for transfers between devices: 274 us -> none  [shards(): grad_q, grad_kv = lax.psum((grad_q, grad_kv), ('own', 'rep'))]
    all_to_all x0 -> x5, blocking collectives: none -> 83.2 us  [exchange(): return lax.all_to_all(blocks, axes, split_axis=0, concat_axis=0, tiled=True)]
    all_to_all x2, starting transfers between devices: 28 us -> 7.18 us  [exchange(): return lax.all_to_all(blocks, axes, split_axis=0, concat_axis=0, tiled=True)]
    all_gather x2 -> x0, blocking collectives: 20.3 us -> none  [the longest x1 10.9 us: shards(): lax.all_gather(node_rows, 'rep', axis=0, tiled=True)]
    scatter-add x2 -> x0, other arithmetic: 15.6 us -> none  [the longest x1 14.2 us: shards(): jax.ops.segment_sum(contrib, edge_ids, num_segments=table_rows)]
    gather x3 -> x0, local copies, waits for them, and re-layouts: 12.4 us -> none  [the longest x2 10.8 us: shards(): jnp.take(keyval, neighbours.reshape(-1), axis=0)]
    mul x2 -> x0, local copies, waits for them, and re-layouts: 10.7 us -> none  [the longest x1 5.37 us: shards(): attention_b.astype(jnp.float32)[..., None]]
    mul x2 -> x0, other arithmetic: 10.1 us -> none  [the longest x1 5.19 us: shards(): attention_b.astype(jnp.float32)[..., None]]
  transfers between devices with their start and end apart: 5 -> 2, of which waited for: 2 -> 2; matrix products, arithmetic and copies ran while one was open for 3% -> 1% of each run, Pallas kernels for 0% -> 0%
where the time goes in v1:
time: 121 us; the launch traced here: 120 us
  blocking collectives  83.2 us (69%)
  waiting for transfers between devices  15.8 us (13%)
  starting transfers between devices  7.18 us (6%)
  Pallas kernels  5.04 us (4%)
  local copies, waits for them, and re-layouts  5 us (4%)
  matrix products  1.96 us (2%)
    all_to_all x5, blocking collectives, exchange(): return lax.all_to_all(blocks, axes, split_axis=0, concat_axis=0, tiled=True)  83.2 us
    all_to_all x2, waiting for transfers between devices, exchange(): return lax.all_to_all(blocks, axes, split_axis=0, concat_axis=0, tiled=True)  15.8 us
    all_to_all x2, starting transfers between devices, exchange(): return lax.all_to_all(blocks, axes, split_axis=0, concat_axis=0, tiled=True)  7.18 us
    pallas_call x1, Pallas kernels, attention(): pl.pallas_call(attention_kernel, out_shape=(jax.ShapeDtypeStruct((nodes,...  5.04 us
    unnamed x17, local copies, waits for them, and re-layouts  2.59 us
  transfers between devices with their start and end apart: 2, of which 2 were waited for; matrix products, arithmetic and copies ran while one was open for 1% of the time, Pallas kernels for 0%

profile of v1, /device:TPU:1, one launch (start us, length us, event | category | flops | bytes accessed | tf_op | source)
XLA Modules:
  0.0 120.1 jit_solution(4239406603469729215)
XLA Ops:
  0.6 0.0 copy-start
  0.6 0.0 copy-start.1
  0.7 0.7 copy-done
  1.3 1.0 fusion.1
  2.4 0.5 broadcast.3
  2.9 0.7 reduce.2
  3.6 29.8 %all_to_all.42 = bf16[128,2,128]{2,1,0:T(2,128)(2,1)S(1)} all-to-all(bf16[128,2,128]{2,1,0:T(2,128)(2,1)S(1)} %reshape.69), channel_id=1, replica_groups=mesh['y'=8,'z'=8,'c'=2,'x'=4] {'y','z','c'}, dimensions={0} | all-to-all | bytes 131072 | tf_op jit(solution)/shard_map/all_to_all | solution.py:30
  33.4 0.0 copy-done.1
  33.4 0.0 copy-start.2
  33.4 0.0 copy-start.3
  33.4 0.0 copy-start.4
  33.4 0.0 copy-start.5
  33.5 12.5 %all_to_all.43 = bf16[4,256,256]{2,1,0:T(8,128)(2,1)S(1)} all-to-all(bf16[4,256,256]{2,1,0:T(8,128)(2,1)S(1)} %broadcast_in_dim.10), channel_id=1, replica_groups=mesh['y'=8,'z'=8,'c'=2,'x'=4] {'x'}, dimensions={0} | all-to-all | bytes 1048576 | tf_op jit(solution)/shard_map/all_to_all | solution.py:30
  46.0 0.0 copy-done.2
  46.0 0.0 copy-done.3
  46.0 0.0 copy-done.4
  46.0 0.0 copy-done.5
  46.0 5.0 %attention.1 = (bf16[128,256]{1,0:T(8,128)(2,1)}, bf16[4,896,128]{2,1,0:T(8,128)(2,1)S(1)}, f32[128,256]{1,0:T(8,128)S(1)}) custom-call(bf16[128,256]{1,0:T(8,128)(2,1)S(1)} %copy-done.1, bf16[128,256]{1,0:T(8,128)(2,1)S(1)} %copy-done.4, s32[16,128]{1,0:T(8,128)S(1)} %bitcast.31, bf16[1024,256]{1,0:T(8,128)(2,1)S(1)} %bitcast.30, ...), custom_call_target="tpu_custom_call" | custom-call | tf_op jit(solution)/shard_map/attention/pallas_call | solution.py:132
  51.1 14.2 %all_to_all.44 = bf16[4,896,128]{2,1,0:T(8,128)(2,1)S(1)} all-to-all(bf16[4,896,128]{2,1,0:T(8,128)(2,1)S(1)} %get-tuple-element.8), channel_id=1, replica_groups=mesh['y'=8,'z'=8,'c'=2,'x'=4] {'x'}, dimensions={0} | all-to-all | bytes 1835008 | tf_op jit(solution)/shard_map/all_to_all | solution.py:30
  65.3 0.1 convert_reduce_fusion
  65.5 15.1 %all_to_all.45 = bf16[16,40,128]{2,1,0:T(8,128)(2,1)S(1)} all-to-all(bf16[16,40,128]{2,1,0:T(8,128)(2,1)S(1)} %pad_maximum_fusion), channel_id=1, replica_groups=mesh['y'=8,'z'=8,'c'=2,'x'=4] {'z','c'}, dimensions={0} | all-to-all | bytes 327680 | tf_op jit(solution)/shard_map/all_to_all | solution.py:30
  80.7 11.6 %all_to_all.46 = bf16[8,56,128]{2,1,0:T(8,128)(2,1)S(1)} all-to-all(bf16[8,56,128]{2,1,0:T(8,128)(2,1)S(1)} %pad_maximum_fusion.2), channel_id=1, replica_groups=mesh['y'=8,'z'=8,'c'=2,'x'=4] {'y'}, dimensions={0} | all-to-all | bytes 229376 | tf_op jit(solution)/shard_map/all_to_all | solution.py:30
  92.4 0.7 broadcast_in_dim.12
  93.0 3.7 %all-to-all-start.5 = ((bf16[16,24,128]{2,1,0:T(8,128)(2,1)}), bf16[16,24,128]{2,1,0:T(8,128)(2,1)S(1)}, u32[]{:S(2)}, u32[]{:S(2)}) async-start(bf16[16,24,128]{2,1,0:T(8,128)(2,1)} %broadcast_in_dim.12), calls=%async_computation.5 | async-start | bytes 196608 | tf_op jit(solution)/shard_map/all_to_all | solution.py:30
  96.8 8.5 %all-to-all-done.5 = bf16[16,24,128]{2,1,0:T(8,128)(2,1)S(1)} async-done(((bf16[16,24,128]{2,1,0:T(8,128)(2,1)}), bf16[16,24,128]{2,1,0:T(8,128)(2,1)S(1)}, u32[]{:S(2)}, u32[]{:S(2)}) %all-to-all-start.5) | async-done | bytes 98336 | tf_op jit(solution)/shard_map/all_to_all | solution.py:30
  105.3 0.8 broadcast_in_dim.14
  106.1 3.5 %all-to-all-start.6 = ((bf16[4,384,128]{2,1,0:T(8,128)(2,1)}), bf16[4,384,128]{2,1,0:T(8,128)(2,1)S(1)}, u32[]{:S(2)}, u32[]{:S(2)}) async-start(bf16[4,384,128]{2,1,0:T(8,128)(2,1)} %broadcast_in_dim.14), calls=%async_computation.6 | async-start | bytes 786432 | tf_op jit(solution)/shard_map/all_to_all | solution.py:30
  109.6 0.9 fusion
  110.5 7.3 %all-to-all-done.6 = bf16[4,384,128]{2,1,0:T(8,128)(2,1)S(1)} async-done(((bf16[4,384,128]{2,1,0:T(8,128)(2,1)}), bf16[4,384,128]{2,1,0:T(8,128)(2,1)S(1)}, u32[]{:S(2)}, u32[]{:S(2)}) %all-to-all-start.6) | async-done | bytes 393248 | tf_op jit(solution)/shard_map/all_to_all | solution.py:30
  117.8 0.1 convert_bitcast_fusion
  117.9 0.3 copy.29
  118.2 1.0 copy.31
  119.2 0.8 copy.30
  (21 shorter events, 0.3 us)
Async XLA Ops:
  0.6 0.7 copy-start
  0.6 32.7 %copy-start.1 = (bf16[128,256]{1,0:T(8,128)(2,1)S(1)}, bf16[128,256]{1,0:T(8,128)(2,1)}, u32[]{:S(2)}) copy-start(bf16[128,256]{1,0:T(8,128)(2,1)} %node_ref.1) | copy-start | bytes 196612
  33.4 12.6 %copy-start.2 = (bf16[256,512]{1,0:T(8,128)(2,1)S(1)}, bf16[256,512]{1,0:T(8,128)(2,1)}, u32[]{:S(2)}) copy-start(bf16[256,512]{1,0:T(8,128)(2,1)} %wkv_ref.1) | copy-start | bytes 786436
  33.4 12.6 %copy-start.3 = (bf16[256,256]{1,0:T(8,128)(2,1)S(1)}, bf16[256,256]{1,0:T(8,128)(2,1)}, u32[]{:S(2)}) copy-start(bf16[256,256]{1,0:T(8,128)(2,1)} %wq_ref.1) | copy-start | bytes 393220
  33.4 12.6 %copy-start.4 = (bf16[128,256]{1,0:T(8,128)(2,1)S(1)}, bf16[128,256]{1,0:T(8,128)(2,1)}, u32[]{:S(2)}) copy-start(bf16[128,256]{1,0:T(8,128)(2,1)} %grad_ref.1) | copy-start | bytes 196612
  33.4 12.6 %copy-start.5 = (s32[128,16]{0,1:T(8,128)S(1)}, s32[128,16]{0,1:T(8,128)}, u32[]{:S(2)}) copy-start(s32[128,16]{0,1:T(8,128)} %param.10) | copy-start | bytes 24580
  93.0 12.2 %all-to-all-start.5 = ((bf16[16,24,128]{2,1,0:T(8,128)(2,1)}), bf16[16,24,128]{2,1,0:T(8,128)(2,1)S(1)}, u32[]{:S(2)}, u32[]{:S(2)}) async-start(bf16[16,24,128]{2,1,0:T(8,128)(2,1)} %broadcast_in_dim.12), calls=%async_computation.5 | async-start | bytes 196608 | tf_op jit(solution)/shard_map/all_to_all | solution.py:30
  106.1 11.7 %all-to-all-start.6 = ((bf16[4,384,128]{2,1,0:T(8,128)(2,1)}), bf16[4,384,128]{2,1,0:T(8,128)(2,1)S(1)}, u32[]{:S(2)}, u32[]{:S(2)}) async-start(bf16[4,384,128]{2,1,0:T(8,128)(2,1)} %broadcast_in_dim.14), calls=%async_computation.6 | async-start | bytes 786432 | tf_op jit(solution)/shard_map/all_to_all | solution.py:30

commit v2 on v1

--- a/solution.py
+++ b/solution.py
@@ -11,6 +11,7 @@
 HEADS = 4
 HEAD_DIM = 64
 LANES = 128
+SMALL = 8 * 1024 * 1024
 BF16, F32 = jnp.bfloat16, jnp.float32
 
 
@@ -40,11 +41,58 @@
     return jnp.concatenate([jnp.where(head == h, wide, 0.0) for h in range(HEADS)], 0)
 
 
+def per_pair(values, weights):
+    wide, long = weights.shape[1] // (HEADS // 2), 2 * HEAD_DIM
+    pairs = [
+        columns_of_both(values[:, p * long : (p + 1) * long], weights[:, p * wide : (p + 1) * wide])
+        for p in range(HEADS // 2)
+    ]
+    return jnp.concatenate(pairs, 0)
+
+
 def own_blocks(table, nodes):
     blocks = [
-        table[h * HEAD_DIM : (h + 1) * HEAD_DIM, h * nodes : (h + 1) * nodes] for h in range(HEADS)
+        table[h * HEAD_DIM : (h + 1) * HEAD_DIM, h % 2 * nodes : (h % 2 + 1) * nodes]
+        for h in range(HEADS)
     ]
     return jnp.concatenate(blocks, 0).T
+
+
+def pick_kernel(rows_ref, node_ref, out_ref, kept_ref):
+    kept_ref[...] = node_ref[...]
+    nodes = node_ref.shape[0]
+    picks = lax.broadcasted_iota(jnp.int32, (nodes, rows_ref.shape[1]), 0) == rows_ref[...]
+    picks = jnp.where(picks, 1.0, 0.0).astype(BF16)
+    out_ref[...] = columns_of_both(picks, node_ref[...]).astype(BF16)
+
+
+def finish_kernel(
+    rows_ref, landed_ref, summed_ref, dnode_ref, grads_ref, attended_in_ref,
+    attended_ref, nodes_ref, grad_q_ref, grad_kv_ref,
+):
+    nodes, features = dnode_ref.shape
+    outer, _, lanes = landed_ref.shape
+    owners = rows_ref.shape[1]
+    inner = owners // outer
+    attended_ref[...] = attended_in_ref[...]
+    each = grads_ref.shape[1]
+    down = features // LANES
+    for piece in range(grads_ref.shape[0] * each // LANES):
+        at = piece % (each // LANES) * LANES
+        block = grads_ref[piece // (each // LANES), at : at + LANES, :].astype(F32)
+        column, row = (piece // down) * LANES, (piece % down) * LANES
+        if column < features:
+            grad_q_ref[row : row + LANES, column : column + LANES] = block
+        else:
+            column = column - features
+            grad_kv_ref[row : row + LANES, column : column + LANES] = block
+    picks = lax.broadcasted_iota(jnp.int32, (nodes, owners), 0) == rows_ref[...]
+    picks = jnp.where(picks, 1.0, 0.0).astype(BF16)
+    for half in range(features // LANES):
+        at = slice(half * LANES, (half + 1) * LANES)
+        back = landed_ref[:, half * inner : (half + 1) * inner, :].reshape(owners, lanes)
+        total = summed_ref[half * nodes : (half + 1) * nodes, :] + dnode_ref[:, at]
+        nodes_ref[:, at] = (total + dot(picks, back)).astype(BF16)
 
 
 def attention_kernel(
@@ -69,16 +117,19 @@
     links = owner * block + jnp.where(arrived, nodes, 0) + links % nodes
 
     keyval = []
+    whole_kv = dot(table_ref[...], wkv).astype(BF16)
     total = jnp.zeros((1, HEADS * nodes), F32)
     inner = jnp.zeros((1, HEADS * nodes), F32)
     for r in range(replicas):
         span = slice(r * block, (r + 1) * block)
-        kv = dot(table_ref[span, :], wkv).astype(BF16)
+        kv = whole_kv[span, :]
         keyval.append(kv)
-        here = lax.broadcasted_iota(jnp.int32, (block, nodes), 0) + r * block
-        count = jnp.zeros((block, nodes), F32)
+        here = (lax.broadcasted_iota(jnp.int32, (block, nodes), 0) + r * block).astype(jnp.int16)
+        count = jnp.zeros((block, nodes), BF16)
         for j in range(degree):
-            count = count + jnp.where(here == links[j : j + 1, :], 1.0, 0.0)
+            hit = here == jnp.broadcast_to(links[j : j + 1, :].astype(jnp.int16), here.shape)
+            count = count + jnp.where(hit, jnp.ones_like(count), jnp.zeros_like(count))
+        count = count.astype(F32)
         log_count = jnp.where(count > 0.0, jnp.log(jnp.maximum(count, 1.0)), -1e30)
         log_count = jnp.concatenate([log_count] * HEADS, 1)
         weight = jnp.exp(rows_of_both(kv[:, :features], q_scaled) + log_count)
@@ -90,19 +141,19 @@
 
     inverse = 1.0 / total
     mean = inner * inverse
-    attended = jnp.zeros((features, HEADS * nodes), F32)
-    dquery = jnp.zeros((features, HEADS * nodes), F32)
-    grad_kv = jnp.zeros(wkv.shape, F32)
+    attended = jnp.zeros((features, 2 * nodes), F32)
+    dquery = jnp.zeros((features, 2 * nodes), F32)
+    all_dkv = []
     for r in range(replicas):
         span = slice(r * block, (r + 1) * block)
         kv = keyval[r]
         prob = weight_scr[span, :] * inverse
         dscore = (prob * (dprob_scr[span, :] - mean)).astype(BF16)
         prob = prob.astype(BF16)
-        attended = attended + columns_of_both(kv[:, features:], prob)
-        dquery = dquery + columns_of_both(kv[:, :features], dscore)
+        attended = attended + per_pair(kv[:, features:], prob)
+        dquery = dquery + per_pair(kv[:, :features], dscore)
         dkv = jnp.concatenate([dot(dscore, q_heads), dot(prob, g_heads)], 1).astype(BF16)
-        grad_kv = grad_kv + columns_of_both(table_ref[span, :], dkv)
+        all_dkv.append(dkv)
         dsrc = rows_of_both(dkv, wkv).astype(BF16)
         for part in range(2):
             for half in range(2):
@@ -111,6 +162,7 @@
                     part * nodes : (part + 1) * nodes, half * LANES : (half + 1) * LANES
                 ]
 
+    grad_kv = columns_of_both(table_ref[...], jnp.concatenate(all_dkv, 0))
     attended_ref[...] = own_blocks(attended, nodes).astype(BF16)
     dquery = own_blocks(dquery, nodes).astype(BF16)
     dnode_ref[...] = rows_of_both(dquery, wq_ref[...])
@@ -152,41 +204,54 @@
 
     wanted = need_rows.reshape(owners, replicas).T
     my_rows = lax.dynamic_index_in_dim(wanted, lax.axis_index("x"), 0, keepdims=False)
-    picks = (my_rows[:, None] == jnp.arange(nodes, dtype=jnp.int32)[None, :]).astype(BF16)
-    outgoing = dot(picks, node_rows).astype(BF16)
-    incoming = exchange(outgoing, ("y", "z", "c"))
-    table = spread(jnp.concatenate([node_rows, incoming], 0), "x", replicas)
+    my_rows = my_rows[None, :]
+    whole = pl.BlockSpec(memory_space=pltpu.VMEM)
+    outgoing, kept = pl.pallas_call(
+        pick_kernel,
+        out_shape=(
+            jax.ShapeDtypeStruct((owners, features), BF16),
+            jax.ShapeDtypeStruct((nodes, features), BF16),
+        ),
+        in_specs=[whole] * 2,
+        out_specs=(whole,) * 2,
+        compiler_params=pltpu.CompilerParams(vmem_limit_bytes=SMALL),
+        name="pick",
+    )(my_rows, node_rows)
+    incoming = exchange(outgoing.reshape(owners, -1, LANES), ("y", "z", "c")).reshape(owners, features)
+    table = spread(jnp.concatenate([kept, incoming], 0), "x", replicas)
     table = table.reshape(-1, features)
 
     attended, partial, dnode = attention(
-        node_rows, grad_out, neighbours.T, table, w_query, w_keyval, replicas
+        kept, grad_out, neighbours.T, table, w_query, w_keyval, replicas
     )
 
     summed = jnp.sum(exchange(partial, "x").astype(F32), 0)
-    own = jnp.concatenate([summed[:nodes], summed[nodes : 2 * nodes]], 1)
     back = summed[2 * nodes : 4 * nodes].astype(BF16).reshape(2, ny, inner, LANES)
     grads = summed[4 * nodes :].astype(BF16).reshape(inner, -1, LANES)
-    kept = grads.shape[1]
+    each = grads.shape[1]
     back = back.transpose(2, 0, 1, 3).reshape(inner, 2 * ny, LANES)
     landed = exchange(jnp.concatenate([back, grads], 1), ("z", "c"))
     back = landed[:, : 2 * ny].reshape(inner, 2, ny, LANES).transpose(2, 1, 0, 3)
     back = back.reshape(ny, 2 * inner, LANES)
     grads = jnp.sum(landed[:, 2 * ny :].astype(F32), 0).astype(BF16)
-    grads = jnp.broadcast_to(grads[None], (ny, kept, LANES))
+    grads = jnp.broadcast_to(grads[None], (ny, each, LANES))
     landed = exchange(jnp.concatenate([back, grads], 1), "y")
-    returned = jnp.concatenate(
-        [
-            landed[:, :inner].reshape(owners, LANES),
-            landed[:, inner : 2 * inner].reshape(owners, LANES),
-        ],
-        1,
-    )
-    grad_nodes = (own + dnode + columns_of_both(picks, returned)).astype(BF16)
     grads = jnp.sum(landed[:, 2 * inner :].astype(F32), 0).astype(BF16)
     grads = spread(grads, ("z", "c"), inner).reshape(-1, LANES)
-    grads = spread(grads, "x", replicas).reshape(-1, features, LANES).astype(F32)
-    grads = grads.transpose(1, 0, 2).reshape(features, -1)
-    return attended, grad_nodes, grads[:, :features], grads[:, features:]
+    grads = spread(grads, "x", replicas)
+    return pl.pallas_call(
+        finish_kernel,
+        out_shape=(
+            jax.ShapeDtypeStruct((nodes, features), BF16),
+            jax.ShapeDtypeStruct((nodes, features), BF16),
+            jax.ShapeDtypeStruct(w_query.shape, F32),
+            jax.ShapeDtypeStruct(w_keyval.shape, F32),
+        ),
+        in_specs=[whole] * 6,
+        out_specs=(whole,) * 4,
+        compiler_params=pltpu.CompilerParams(vmem_limit_bytes=SMALL),
+        name="finish",
+    )(my_rows, landed, summed, dnode, grads, attended)
 
 
 def solution(mesh):

time: 121 us -> 113 us (0.934)
  blocking collectives: 83.2 us -> 105 us
  waiting for transfers between devices: 15.8 us -> 0 us
  starting transfers between devices: 7.18 us -> 0 us
  local copies, waits for them, and re-layouts: 5 us -> 1.75 us
  matrix products: 1.96 us -> 0 us
    all_to_all x5 -> x7, blocking collectives: 83.2 us -> 105 us  [exchange(): return lax.all_to_all(blocks, axes, split_axis=0, concat_axis=0, tiled=True)]
    all_to_all x2 -> x0, waiting for transfers between devices: 15.8 us -> none  [exchange(): return lax.all_to_all(blocks, axes, split_axis=0, concat_axis=0, tiled=True)]
    all_to_all x2 -> x0, starting transfers between devices: 7.18 us -> none  [exchange(): return lax.all_to_all(blocks, axes, split_axis=0, concat_axis=0, tiled=True)]
    dot_general x2 -> x0, matrix products: 1.96 us -> none  [dot(): lax.dot_general(a, b, (contract, ((), ())), preferred_element_type=F32)]
    pallas_call x1, Pallas kernels: 5.04 us -> 3.33 us  [attention(): pl.pallas_call(attention_kernel, out_shape=(jax.ShapeDtypeStruct((nodes,...]
    broadcast_in_dim x3, local copies, waits for them, and re-layouts: 1.49 us -> 0.1 us  [spread(): return exchange(jnp.broadcast_to(block[None], (count,) + block.shape), axes)]
    unnamed x17 -> x13, local copies, waits for them, and re-layouts: 2.59 us -> 1.55 us
  transfers between devices with their start and end apart: 2 -> 0, of which waited for: 2 -> 0; matrix products, arithmetic and copies ran while one was open for 1% -> 0% of each run, Pallas kernels for 0% -> 0%
where the time goes in v2:
time: 113 us
  blocking collectives  105 us (93%)
  Pallas kernels  4.53 us (4%)
  local copies, waits for them, and re-layouts  1.75 us (2%)
    all_to_all x7, blocking collectives, exchange(): return lax.all_to_all(blocks, axes, split_axis=0, concat_axis=0, tiled=True)  105 us
    pallas_call x1, Pallas kernels, attention(): pl.pallas_call(attention_kernel, out_shape=(jax.ShapeDtypeStruct((nodes,...  3.33 us

profile of v2, /device:TPU:1, one launch (start us, length us, event | category | flops | bytes accessed | tf_op | source)
XLA Modules:
  0.0 112.6 jit_solution(6637915975892953831)
XLA Ops:
  0.6 0.0 copy-start
  0.6 0.7 copy-done
  1.3 0.0 copy-start.4
  1.3 0.8 copy-done.4
  2.2 0.2 pick.1
  2.4 29.7 %all_to_all.35 = bf16[128,2,128]{2,1,0:T(2,128)(2,1)S(1)} all-to-all(bf16[128,2,128]{2,1,0:T(2,128)(2,1)S(1)} %reshape.40), channel_id=1, replica_groups=mesh['y'=8,'z'=8,'c'=2,'x'=4] {'y','z','c'}, dimensions={0} | all-to-all | bytes 131072 | tf_op jit(solution)/shard_map/all_to_all | solution.py:31
  32.2 0.0 copy-start.1
  32.2 0.0 copy-start.2
  32.2 0.0 copy-start.3
  32.2 0.0 copy-start.5
  32.3 12.5 %all_to_all.36 = bf16[4,256,256]{2,1,0:T(8,128)(2,1)S(1)} all-to-all(bf16[4,256,256]{2,1,0:T(8,128)(2,1)S(1)} %broadcast_in_dim.10), channel_id=1, replica_groups=mesh['y'=8,'z'=8,'c'=2,'x'=4] {'x'}, dimensions={0} | all-to-all | bytes 1048576 | tf_op jit(solution)/shard_map/all_to_all | solution.py:31
  44.8 0.0 copy-done.1
  44.8 0.0 copy-done.2
  44.8 0.0 copy-done.3
  44.8 0.0 copy-done.5
  44.8 3.3 %attention.1 = (bf16[128,256]{1,0:T(8,128)(2,1)S(1)}, bf16[4,896,128]{2,1,0:T(8,128)(2,1)S(1)}, f32[128,256]{1,0:T(8,128)S(1)}) custom-call(bf16[128,256]{1,0:T(8,128)(2,1)S(1)} %get-tuple-element.9.node_ref, bf16[128,256]{1,0:T(8,128)(2,1)S(1)} %copy-done.3, s32[16,128]{1,0:T(8,128)S(1)} %bitcast.22, bf16[1024,256]{1,0:T(8,128)(2,1)S(1)} %bitcast.21, ...), custom_call_target="tpu_custom_call" | custom-call | tf_op jit(solution)/shard_map/attention/pallas_call | solution.py:184
  48.1 14.3 %all_to_all.37 = bf16[4,896,128]{2,1,0:T(8,128)(2,1)S(1)} all-to-all(bf16[4,896,128]{2,1,0:T(8,128)(2,1)S(1)} %get-tuple-element.11), channel_id=1, replica_groups=mesh['y'=8,'z'=8,'c'=2,'x'=4] {'x'}, dimensions={0} | all-to-all | bytes 1835008 | tf_op jit(solution)/shard_map/all_to_all | solution.py:31
  62.4 0.1 convert_reduce_fusion.summed_ref
  62.6 15.1 %all_to_all.38 = bf16[16,40,128]{2,1,0:T(8,128)(2,1)S(1)} all-to-all(bf16[16,40,128]{2,1,0:T(8,128)(2,1)S(1)} %pad_maximum_fusion), channel_id=1, replica_groups=mesh['y'=8,'z'=8,'c'=2,'x'=4] {'z','c'}, dimensions={0} | all-to-all | bytes 327680 | tf_op jit(solution)/shard_map/all_to_all | solution.py:31
  77.8 11.6 %all_to_all.39.landed_ref = bf16[8,56,128]{2,1,0:T(8,128)(2,1)S(1)} all-to-all(bf16[8,56,128]{2,1,0:T(8,128)(2,1)S(1)} %pad_maximum_fusion.2), channel_id=1, replica_groups=mesh['y'=8,'z'=8,'c'=2,'x'=4] {'y'}, dimensions={0} | all-to-all | bytes 229376 | tf_op jit(solution)/shard_map/all_to_all | solution.py:31
  89.5 11.3 %all_to_all.40 = bf16[16,24,128]{2,1,0:T(8,128)(2,1)S(1)} all-to-all(bf16[16,24,128]{2,1,0:T(8,128)(2,1)S(1)} %broadcast_in_dim.12), channel_id=1, replica_groups=mesh['y'=8,'z'=8,'c'=2,'x'=4] {'z','c'}, dimensions={0} | all-to-all | bytes 196608 | tf_op jit(solution)/shard_map/all_to_all | solution.py:31
  100.8 0.1 broadcast_in_dim.14
  100.9 10.7 %all_to_all.41.grads_ref = bf16[4,384,128]{2,1,0:T(8,128)(2,1)S(1)} all-to-all(bf16[4,384,128]{2,1,0:T(8,128)(2,1)S(1)} %broadcast_in_dim.14), channel_id=1, replica_groups=mesh['y'=8,'z'=8,'c'=2,'x'=4] {'x'}, dimensions={0} | all-to-all | bytes 786432 | tf_op jit(solution)/shard_map/all_to_all | solution.py:31
  111.6 1.0 finish.1
  (17 shorter events, 0.3 us)
Async XLA Ops:
  0.6 0.7 copy-start
  1.3 0.8 copy-start.4
  32.2 12.6 %copy-start.1 = (bf16[256,512]{1,0:T(8,128)(2,1)S(1)}, bf16[256,512]{1,0:T(8,128)(2,1)}, u32[]{:S(2)}) copy-start(bf16[256,512]{1,0:T(8,128)(2,1)} %wkv_ref.1) | copy-start | bytes 786436
  32.2 12.6 %copy-start.2 = (bf16[256,256]{1,0:T(8,128)(2,1)S(1)}, bf16[256,256]{1,0:T(8,128)(2,1)}, u32[]{:S(2)}) copy-start(bf16[256,256]{1,0:T(8,128)(2,1)} %wq_ref.1) | copy-start | bytes 393220
  32.2 12.6 %copy-start.3 = (bf16[128,256]{1,0:T(8,128)(2,1)S(1)}, bf16[128,256]{1,0:T(8,128)(2,1)}, u32[]{:S(2)}) copy-start(bf16[128,256]{1,0:T(8,128)(2,1)} %grad_ref.1) | copy-start | bytes 196612
  32.2 12.6 %copy-start.5 = (s32[128,16]{0,1:T(8,128)S(1)}, s32[128,16]{0,1:T(8,128)}, u32[]{:S(2)}) copy-start(s32[128,16]{0,1:T(8,128)} %param.10) | copy-start | bytes 24580

commit v3 on v2

--- a/solution.py
+++ b/solution.py
@@ -1,3 +1,4 @@
+import itertools
 import math
 
 import jax
@@ -67,27 +68,30 @@
 
 
 def finish_kernel(
-    rows_ref, landed_ref, summed_ref, dnode_ref, grads_ref, attended_in_ref,
+    core_ref, rows_ref, landed_ref, summed_ref, dnode_ref, mine_ref, other_ref, attended_in_ref,
     attended_ref, nodes_ref, grad_q_ref, grad_kv_ref,
 ):
     nodes, features = dnode_ref.shape
     outer, _, lanes = landed_ref.shape
     owners = rows_ref.shape[1]
     inner = owners // outer
+    cores = 2
     attended_ref[...] = attended_in_ref[...]
-    each = grads_ref.shape[1]
-    down = features // LANES
-    for piece in range(grads_ref.shape[0] * each // LANES):
-        at = piece % (each // LANES) * LANES
-        block = grads_ref[piece // (each // LANES), at : at + LANES, :].astype(F32)
-        column, row = (piece // down) * LANES, (piece % down) * LANES
-        if column < features:
-            grad_q_ref[row : row + LANES, column : column + LANES] = block
-        else:
-            column = column - features
-            grad_kv_ref[row : row + LANES, column : column + LANES] = block
+    replicas, depth, each, _ = mine_ref.shape
+    for x, z, c in itertools.product(range(replicas), range(depth), range(cores)):
+        block = jnp.where(core_ref[0] == c, mine_ref[x, z], other_ref[x, z]).astype(F32)
+        first = ((x * cores + c) * depth + z) * each
+        for row in range(first, first + each, 8):
+            column, at = row // features * LANES, row % features
+            to_ref = grad_q_ref if column < features else grad_kv_ref
+            column = column if column < features else column - features
+            to_ref[at : at + 8, column : column + LANES] = block[row - first : row - first + 8]
     picks = lax.broadcasted_iota(jnp.int32, (nodes, owners), 0) == rows_ref[...]
     picks = jnp.where(picks, 1.0, 0.0).astype(BF16)
+    given = lax.broadcasted_iota(jnp.int32, (owners, owners), 0)
+    asked = lax.broadcasted_iota(jnp.int32, (owners, owners), 1)
+    asked = asked // inner * inner + asked % depth * cores + asked // depth % cores
+    picks = dot(picks, jnp.where(given == asked, 1.0, 0.0).astype(BF16)).astype(BF16)
     for half in range(features // LANES):
         at = slice(half * LANES, (half + 1) * LANES)
         back = landed_ref[:, half * inner : (half + 1) * inner, :].reshape(owners, lanes)
@@ -226,19 +230,21 @@
     )
 
     summed = jnp.sum(exchange(partial, "x").astype(F32), 0)
-    back = summed[2 * nodes : 4 * nodes].astype(BF16).reshape(2, ny, inner, LANES)
+    back = summed[2 * nodes : 4 * nodes].astype(BF16).reshape(2, ny, nz, nc, LANES)
     grads = summed[4 * nodes :].astype(BF16).reshape(inner, -1, LANES)
     each = grads.shape[1]
-    back = back.transpose(2, 0, 1, 3).reshape(inner, 2 * ny, LANES)
-    landed = exchange(jnp.concatenate([back, grads], 1), ("z", "c"))
+    back = back.transpose(3, 2, 0, 1, 4).reshape(inner, 2 * ny, LANES)
+    landed = exchange(jnp.concatenate([back, grads], 1), ("c", "z"))
     back = landed[:, : 2 * ny].reshape(inner, 2, ny, LANES).transpose(2, 1, 0, 3)
     back = back.reshape(ny, 2 * inner, LANES)
     grads = jnp.sum(landed[:, 2 * ny :].astype(F32), 0).astype(BF16)
     grads = jnp.broadcast_to(grads[None], (ny, each, LANES))
     landed = exchange(jnp.concatenate([back, grads], 1), "y")
     grads = jnp.sum(landed[:, 2 * inner :].astype(F32), 0).astype(BF16)
-    grads = spread(grads, ("z", "c"), inner).reshape(-1, LANES)
-    grads = spread(grads, "x", replicas)
+    grads = spread(grads, ("x", "z"), nz * replicas)
+    grads = grads.reshape(replicas, nz, each, LANES)
+    other = lax.ppermute(grads, "c", [(0, 1), (1, 0)])
+    core = lax.axis_index("c").reshape(1)
     return pl.pallas_call(
         finish_kernel,
         out_shape=(
@@ -247,11 +253,11 @@
             jax.ShapeDtypeStruct(w_query.shape, F32),
             jax.ShapeDtypeStruct(w_keyval.shape, F32),
         ),
-        in_specs=[whole] * 6,
+        in_specs=[pl.BlockSpec(memory_space=pltpu.SMEM)] + [whole] * 7,
         out_specs=(whole,) * 4,
         compiler_params=pltpu.CompilerParams(vmem_limit_bytes=SMALL),
         name="finish",
-    )(my_rows, landed, summed, dnode, grads, attended)
+    )(core, my_rows, landed, summed, dnode, grads, other, attended)
 
 
 def solution(mesh):

time: 113 us -> 109 us (0.965)
  blocking collectives: 105 us -> 95 us
  starting transfers between devices: 0 us -> 4.74 us
    all_to_all x7 -> x6, blocking collectives: 105 us -> 95 us  [exchange(): return lax.all_to_all(blocks, axes, split_axis=0, concat_axis=0, tiled=True)]
    ppermute x0 -> x1, starting transfers between devices: none -> 4.74 us  [shards(): other = lax.ppermute(grads, 'c', [(0, 1), (1, 0)])]
  transfers between devices with their start and end apart: 0 -> 1, of which waited for: 0 -> 1; matrix products, arithmetic and copies ran while one was open for 0% -> 0% of each run, Pallas kernels for 0% -> 0%
where the time goes in v3:
time: 109 us; the launch traced here: 108 us
  blocking collectives  95 us (87%)
  starting transfers between devices  4.74 us (4%)
  Pallas kernels  4.71 us (4%)
  local copies, waits for them, and re-layouts  1.71 us (2%)
    all_to_all x6, blocking collectives, exchange(): return lax.all_to_all(blocks, axes, split_axis=0, concat_axis=0, tiled=True)  95 us
    ppermute x1, starting transfers between devices, shards(): other = lax.ppermute(grads, 'c', [(0, 1), (1, 0)])  4.74 us
    pallas_call x1, Pallas kernels, attention(): pl.pallas_call(attention_kernel, out_shape=(jax.ShapeDtypeStruct((nodes,...  3.33 us
  transfers between devices with their start and end apart: 1, of which 1 were waited for; matrix products, arithmetic and copies ran while one was open for 0% of the time, Pallas kernels for 0%

profile of v3, /device:TPU:1, one launch (start us, length us, event | category | flops | bytes accessed | tf_op | source)
XLA Modules:
  0.0 108.2 jit_solution(12172340033258345219)
XLA Ops:
  0.6 0.0 copy-start
  0.6 0.7 copy-done
  1.3 0.0 copy-start.4
  1.3 0.8 copy-done.4
  2.2 0.2 pick.1
  2.4 29.7 %all_to_all.30 = bf16[128,2,128]{2,1,0:T(2,128)(2,1)S(1)} all-to-all(bf16[128,2,128]{2,1,0:T(2,128)(2,1)S(1)} %reshape.46), channel_id=1, replica_groups=mesh['y'=8,'z'=8,'c'=2,'x'=4] {'y','z','c'}, dimensions={0} | all-to-all | bytes 131072 | tf_op jit(solution)/shard_map/all_to_all | solution.py:32
  32.2 0.0 copy-start.1
  32.2 0.0 copy-start.2
  32.2 0.0 copy-start.3
  32.2 0.0 copy-start.5
  32.3 12.5 %all_to_all.31 = bf16[4,256,256]{2,1,0:T(8,128)(2,1)S(1)} all-to-all(bf16[4,256,256]{2,1,0:T(8,128)(2,1)S(1)} %broadcast_in_dim.6), channel_id=1, replica_groups=mesh['y'=8,'z'=8,'c'=2,'x'=4] {'x'}, dimensions={0} | all-to-all | bytes 1048576 | tf_op jit(solution)/shard_map/all_to_all | solution.py:32
  44.8 0.0 copy-done.1
  44.8 0.0 copy-done.2
  44.8 0.0 copy-done.3
  44.8 0.0 copy-done.5
  44.8 3.3 %attention.1 = (bf16[128,256]{1,0:T(8,128)(2,1)S(1)}, bf16[4,896,128]{2,1,0:T(8,128)(2,1)S(1)}, f32[128,256]{1,0:T(8,128)S(1)}) custom-call(bf16[128,256]{1,0:T(8,128)(2,1)S(1)} %get-tuple-element.9.node_ref, bf16[128,256]{1,0:T(8,128)(2,1)S(1)} %copy-done.3, s32[16,128]{1,0:T(8,128)S(1)} %bitcast.23, bf16[1024,256]{1,0:T(8,128)(2,1)S(1)} %bitcast.20, ...), custom_call_target="tpu_custom_call" | custom-call | tf_op jit(solution)/shard_map/attention/pallas_call | solution.py:188
  48.1 14.3 %all_to_all.32 = bf16[4,896,128]{2,1,0:T(8,128)(2,1)S(1)} all-to-all(bf16[4,896,128]{2,1,0:T(8,128)(2,1)S(1)} %get-tuple-element.11), channel_id=1, replica_groups=mesh['y'=8,'z'=8,'c'=2,'x'=4] {'x'}, dimensions={0} | all-to-all | bytes 1835008 | tf_op jit(solution)/shard_map/all_to_all | solution.py:32
  62.4 0.1 convert_reduce_fusion.summed_ref
  62.6 13.1 %all_to_all.33 = bf16[16,40,128]{2,1,0:T(8,128)(2,1)S(1)} all-to-all(bf16[16,40,128]{2,1,0:T(8,128)(2,1)S(1)} %pad_maximum_fusion), channel_id=1, replica_groups=mesh['y'=8,'z'=8,'c'=2,'x'=4] {'c','z'}, dimensions={0} | all-to-all | bytes 327680 | tf_op jit(solution)/shard_map/all_to_all | solution.py:32
  75.8 10.1 %all_to_all.34.landed_ref = bf16[8,56,128]{2,1,0:T(8,128)(2,1)S(1)} all-to-all(bf16[8,56,128]{2,1,0:T(8,128)(2,1)S(1)} %pad_maximum_fusion.2), channel_id=1, replica_groups=mesh['y'=8,'z'=8,'c'=2,'x'=4] {'y'}, dimensions={0} | all-to-all | bytes 229376 | tf_op jit(solution)/shard_map/all_to_all | solution.py:32
  86.0 15.3 %all_to_all.35 = bf16[32,24,128]{2,1,0:T(8,128)(2,1)S(1)} all-to-all(bf16[32,24,128]{2,1,0:T(8,128)(2,1)S(1)} %broadcast_in_dim.8), channel_id=1, replica_groups=mesh['y'=8,'z'=8,'c'=2,'x'=4] {'x','z'}, dimensions={0} | all-to-all | bytes 393216 | tf_op jit(solution)/shard_map/all_to_all | solution.py:32
  101.2 4.7 %collective-permute-start = (bf16[4,8,24,128]{3,2,1,0:T(8,128)(2,1)S(1)}, bf16[4,8,24,128]{3,2,1,0:T(8,128)(2,1)S(1)}, u32[]{:S(2)}, u32[]{:S(2)}) collective-permute-start(bf16[4,8,24,128]{3,2,1,0:T(8,128)(2,1)S(1)} %bitcast.21), channel_id=1, source_target_pairs={{0,4},{4,0},{1,5},{5,1},{2,6},{6,2},{3,7},{7,3},{8,12},{12,8},{9,1... | collective-permute-start | bytes 589832 | tf_op jit(solution)/shard_map/ppermute | solution.py:246
  106.0 1.0 collective-permute-done.other_ref
  107.0 1.2 %finish.1 = (bf16[128,256]{1,0:T(8,128)(2,1)}, bf16[128,256]{1,0:T(8,128)(2,1)}, f32[256,256]{1,0:T(8,128)}, f32[256,512]{1,0:T(8,128)}) custom-call(s32[1]{0:T(128)} %bitcast.core_ref, s32[1,128]{1,0:T(1,128)S(1)} %dynamic-slice_bitcast_fusion.rows_ref, bf16[8,56,128]{2,1,0:T(8,128)(2,1)S(1)} %all_to_all.34.landed_ref, ...), custom_call_target="tpu_custom_call" | custom-call | tf_op jit(solution)/shard_map/finish/pallas_call | solution.py:248
  (17 shorter events, 0.3 us)
Async XLA Ops:
  0.6 0.7 copy-start
  1.3 0.8 copy-start.4
  32.2 12.6 %copy-start.1 = (bf16[256,512]{1,0:T(8,128)(2,1)S(1)}, bf16[256,512]{1,0:T(8,128)(2,1)}, u32[]{:S(2)}) copy-start(bf16[256,512]{1,0:T(8,128)(2,1)} %wkv_ref.1) | copy-start | bytes 786436
  32.2 12.6 %copy-start.2 = (bf16[256,256]{1,0:T(8,128)(2,1)S(1)}, bf16[256,256]{1,0:T(8,128)(2,1)}, u32[]{:S(2)}) copy-start(bf16[256,256]{1,0:T(8,128)(2,1)} %wq_ref.1) | copy-start | bytes 393220
  32.2 12.6 %copy-start.3 = (bf16[128,256]{1,0:T(8,128)(2,1)S(1)}, bf16[128,256]{1,0:T(8,128)(2,1)}, u32[]{:S(2)}) copy-start(bf16[128,256]{1,0:T(8,128)(2,1)} %grad_ref.1) | copy-start | bytes 196612
  32.2 12.6 %copy-start.5 = (s32[128,16]{0,1:T(8,128)S(1)}, s32[128,16]{0,1:T(8,128)}, u32[]{:S(2)}) copy-start(s32[128,16]{0,1:T(8,128)} %param.10) | copy-start | bytes 24580
  101.2 5.8 %collective-permute-start = (bf16[4,8,24,128]{3,2,1,0:T(8,128)(2,1)S(1)}, bf16[4,8,24,128]{3,2,1,0:T(8,128)(2,1)S(1)}, u32[]{:S(2)}, u32[]{:S(2)}) collective-permute-start(bf16[4,8,24,128]{3,2,1,0:T(8,128)(2,1)S(1)} %bitcast.21), channel_id=1, source_target_pairs={{0,4},{4,0},{1,5},{5,1},{2,6},{6,2},{3,7},{7,3},{8,12},{12,8},{9,1... | collective-permute-start | bytes 589832 | tf_op jit(solution)/shard_map/ppermute | solution.py:246

commit v4 on v3

--- a/solution.py
+++ b/solution.py
@@ -12,6 +12,7 @@
 HEADS = 4
 HEAD_DIM = 64
 LANES = 128
+CORES = 2
 SMALL = 8 * 1024 * 1024
 BF16, F32 = jnp.bfloat16, jnp.float32
 
@@ -67,36 +68,37 @@
     out_ref[...] = columns_of_both(picks, node_ref[...]).astype(BF16)
 
 
-def finish_kernel(
-    core_ref, rows_ref, landed_ref, summed_ref, dnode_ref, mine_ref, other_ref, attended_in_ref,
-    attended_ref, nodes_ref, grad_q_ref, grad_kv_ref,
-):
+def node_kernel(rows_ref, landed_ref, summed_ref, dnode_ref, attended_in_ref, attended_ref, nodes_ref):
     nodes, features = dnode_ref.shape
     outer, _, lanes = landed_ref.shape
     owners = rows_ref.shape[1]
     inner = owners // outer
-    cores = 2
+    depth = inner // CORES
     attended_ref[...] = attended_in_ref[...]
-    replicas, depth, each, _ = mine_ref.shape
-    for x, z, c in itertools.product(range(replicas), range(depth), range(cores)):
-        block = jnp.where(core_ref[0] == c, mine_ref[x, z], other_ref[x, z]).astype(F32)
-        first = ((x * cores + c) * depth + z) * each
-        for row in range(first, first + each, 8):
-            column, at = row // features * LANES, row % features
-            to_ref = grad_q_ref if column < features else grad_kv_ref
-            column = column if column < features else column - features
-            to_ref[at : at + 8, column : column + LANES] = block[row - first : row - first + 8]
     picks = lax.broadcasted_iota(jnp.int32, (nodes, owners), 0) == rows_ref[...]
     picks = jnp.where(picks, 1.0, 0.0).astype(BF16)
     given = lax.broadcasted_iota(jnp.int32, (owners, owners), 0)
     asked = lax.broadcasted_iota(jnp.int32, (owners, owners), 1)
-    asked = asked // inner * inner + asked % depth * cores + asked // depth % cores
+    asked = asked // inner * inner + asked % depth * CORES + asked // depth % CORES
     picks = dot(picks, jnp.where(given == asked, 1.0, 0.0).astype(BF16)).astype(BF16)
     for half in range(features // LANES):
         at = slice(half * LANES, (half + 1) * LANES)
         back = landed_ref[:, half * inner : (half + 1) * inner, :].reshape(owners, lanes)
         total = summed_ref[half * nodes : (half + 1) * nodes, :] + dnode_ref[:, at]
         nodes_ref[:, at] = (total + dot(picks, back)).astype(BF16)
+
+
+def weight_kernel(core_ref, mine_ref, other_ref, grad_q_ref, grad_kv_ref):
+    features = grad_q_ref.shape[0]
+    replicas, depth, each, _ = mine_ref.shape
+    for x, z, c in itertools.product(range(replicas), range(depth), range(CORES)):
+        block = jnp.where(core_ref[0] == c, mine_ref[x, z], other_ref[x, z]).astype(F32)
+        first = ((x * CORES + c) * depth + z) * each
+        for row in range(first, first + each, 8):
+            column, at = row // features * LANES, row % features
+            to_ref = grad_q_ref if column < features else grad_kv_ref
+            column = column if column < features else column - features
+            to_ref[at : at + 8, column : column + LANES] = block[row - first : row - first + 8]
 
 
 def attention_kernel(
@@ -222,8 +224,7 @@
         name="pick",
     )(my_rows, node_rows)
     incoming = exchange(outgoing.reshape(owners, -1, LANES), ("y", "z", "c")).reshape(owners, features)
-    table = spread(jnp.concatenate([kept, incoming], 0), "x", replicas)
-    table = table.reshape(-1, features)
+    table = lax.all_gather(jnp.concatenate([kept, incoming], 0), "x", axis=0, tiled=True)
 
     attended, partial, dnode = attention(
         kept, grad_out, neighbours.T, table, w_query, w_keyval, replicas
@@ -245,19 +246,26 @@
     grads = grads.reshape(replicas, nz, each, LANES)
     other = lax.ppermute(grads, "c", [(0, 1), (1, 0)])
     core = lax.axis_index("c").reshape(1)
-    return pl.pallas_call(
-        finish_kernel,
+    attended, grad_nodes = pl.pallas_call(
+        node_kernel,
+        out_shape=(jax.ShapeDtypeStruct((nodes, features), BF16),) * 2,
+        in_specs=[whole] * 5,
+        out_specs=(whole,) * 2,
+        compiler_params=pltpu.CompilerParams(vmem_limit_bytes=SMALL),
+        name="node_sums",
+    )(my_rows, landed, summed, dnode, attended)
+    grad_query, grad_keyval = pl.pallas_call(
+        weight_kernel,
         out_shape=(
-            jax.ShapeDtypeStruct((nodes, features), BF16),
-            jax.ShapeDtypeStruct((nodes, features), BF16),
             jax.ShapeDtypeStruct(w_query.shape, F32),
             jax.ShapeDtypeStruct(w_keyval.shape, F32),
         ),
-        in_specs=[pl.BlockSpec(memory_space=pltpu.SMEM)] + [whole] * 7,
-        out_specs=(whole,) * 4,
+        in_specs=[pl.BlockSpec(memory_space=pltpu.SMEM)] + [whole] * 2,
+        out_specs=(whole,) * 2,
         compiler_params=pltpu.CompilerParams(vmem_limit_bytes=SMALL),
-        name="finish",
-    )(core, my_rows, landed, summed, dnode, grads, other, attended)
+        name="weight_gradients",
+    )(core, grads, other)
+    return attended, grad_nodes, grad_query, grad_keyval
 
 
 def solution(mesh):

time: 109 us -> 107 us (0.982)
  blocking collectives: 95 us -> 93.9 us
    all_to_all x6 -> x5, blocking collectives: 95 us -> 82.5 us  [exchange(): return lax.all_to_all(blocks, axes, split_axis=0, concat_axis=0, tiled=True)]
    all_gather x0 -> x1, blocking collectives: none -> 11.4 us  [shards(): lax.all_gather(jnp.concatenate([kept, incoming], 0), 'x', axis=0, tiled=T...]
  transfers between devices with their start and end apart: 1 -> 1, of which waited for: 1 -> 1; matrix products, arithmetic and copies ran while one was open for 0% -> 0% of each run, Pallas kernels for 0% -> 1%
where the time goes in v4:
time: 107 us
  blocking collectives  93.9 us (88%)
  Pallas kernels  5.4 us (5%)
  starting transfers between devices  4.74 us (4%)
  local copies, waits for them, and re-layouts  1.63 us (2%)
    all_to_all x5, blocking collectives, exchange(): return lax.all_to_all(blocks, axes, split_axis=0, concat_axis=0, tiled=True)  82.5 us
    all_gather x1, blocking collectives, shards(): lax.all_gather(jnp.concatenate([kept, incoming], 0), 'x', axis=0, tiled=T...  11.4 us
    ppermute x1, starting transfers between devices, shards(): other = lax.ppermute(grads, 'c', [(0, 1), (1, 0)])  4.74 us
    pallas_call x1, Pallas kernels, attention(): pl.pallas_call(attention_kernel, out_shape=(jax.ShapeDtypeStruct((nodes,...  3.36 us
  transfers between devices with their start and end apart: 1, of which 1 were waited for; matrix products, arithmetic and copies ran while one was open for 0% of the time, Pallas kernels for 1%

profile of v4, /device:TPU:1, one launch (start us, length us, event | category | flops | bytes accessed | tf_op | source)
XLA Modules:
  0.0 106.8 jit_solution(10627901290834496368)
XLA Ops:
  0.6 0.0 copy-start
  0.6 0.0 copy-start.3
  0.7 0.0 copy-start.1
  0.7 0.0 copy-start.2
  0.7 0.6 copy-done
  1.3 0.0 copy-start.4
  1.3 0.8 copy-done.4
  2.2 0.0 copy-start.5
  2.2 0.2 pick.1
  2.4 29.7 %all_to_all.25 = bf16[128,2,128]{2,1,0:T(2,128)(2,1)S(1)} all-to-all(bf16[128,2,128]{2,1,0:T(2,128)(2,1)S(1)} %reshape.41), channel_id=1, replica_groups=mesh['y'=8,'z'=8,'c'=2,'x'=4] {'y','z','c'}, dimensions={0} | all-to-all | bytes 131072 | tf_op jit(solution)/shard_map/all_to_all | solution.py:33
  32.2 11.4 %all_gather.3.table_ref = bf16[1024,256]{1,0:T(8,128)(2,1)S(1)} all-gather(bf16[256,256]{1,0:T(8,128)(2,1)S(1)} %pad_maximum_fusion.1), channel_id=1, replica_groups=mesh['y'=8,'z'=8,'c'=2,'x'=4] {'x'}, dimensions={0}, use_global_device_ids=true | all-gather | bytes 655360 | tf_op jit(solution)/shard_map/all_gather | solution.py:227
  43.6 0.0 copy-done.3
  43.6 0.0 copy-done.1
  43.6 0.0 copy-done.2
  43.6 0.0 copy-done.5
  43.6 3.4 %attention.1 = (bf16[128,256]{1,0:T(8,128)(2,1)S(1)}, bf16[4,896,128]{2,1,0:T(8,128)(2,1)S(1)}, f32[128,256]{1,0:T(8,128)S(1)}) custom-call(bf16[128,256]{1,0:T(8,128)(2,1)S(1)} %get-tuple-element.13.node_ref, bf16[128,256]{1,0:T(8,128)(2,1)S(1)} %copy-done.3, s32[16,128]{1,0:T(8,128)S(1)} %bitcast.21, bf16[1024,256]{1,0:T(8,128)(2,1)S(1)} %all_gather.3.table_ref, ...), custom_call_target="tpu_custom_call" | custom-call | tf_op jit(solution)/shard_map/attention/pallas_call | solution.py:190
  47.0 12.1 %all_to_all.26 = bf16[4,896,128]{2,1,0:T(8,128)(2,1)S(1)} all-to-all(bf16[4,896,128]{2,1,0:T(8,128)(2,1)S(1)} %get-tuple-element.15), channel_id=1, replica_groups=mesh['y'=8,'z'=8,'c'=2,'x'=4] {'x'}, dimensions={0} | all-to-all | bytes 1835008 | tf_op jit(solution)/shard_map/all_to_all | solution.py:33
  59.1 0.1 convert_reduce_fusion.summed_ref
  59.4 15.2 %all_to_all.27 = bf16[16,40,128]{2,1,0:T(8,128)(2,1)S(1)} all-to-all(bf16[16,40,128]{2,1,0:T(8,128)(2,1)S(1)} %pad_maximum_fusion), channel_id=1, replica_groups=mesh['y'=8,'z'=8,'c'=2,'x'=4] {'c','z'}, dimensions={0} | all-to-all | bytes 327680 | tf_op jit(solution)/shard_map/all_to_all | solution.py:33
  74.6 10.0 %all_to_all.28.landed_ref = bf16[8,56,128]{2,1,0:T(8,128)(2,1)S(1)} all-to-all(bf16[8,56,128]{2,1,0:T(8,128)(2,1)S(1)} %pad_maximum_fusion.2), channel_id=1, replica_groups=mesh['y'=8,'z'=8,'c'=2,'x'=4] {'y'}, dimensions={0} | all-to-all | bytes 229376 | tf_op jit(solution)/shard_map/all_to_all | solution.py:33
  84.7 15.4 %all_to_all.29 = bf16[32,24,128]{2,1,0:T(8,128)(2,1)S(1)} all-to-all(bf16[32,24,128]{2,1,0:T(8,128)(2,1)S(1)} %broadcast_in_dim.5), channel_id=1, replica_groups=mesh['y'=8,'z'=8,'c'=2,'x'=4] {'x','z'}, dimensions={0} | all-to-all | bytes 393216 | tf_op jit(solution)/shard_map/all_to_all | solution.py:33
  100.1 4.7 %collective-permute-start = (bf16[4,8,24,128]{3,2,1,0:T(8,128)(2,1)S(1)}, bf16[4,8,24,128]{3,2,1,0:T(8,128)(2,1)S(1)}, u32[]{:S(2)}, u32[]{:S(2)}) collective-permute-start(bf16[4,8,24,128]{3,2,1,0:T(8,128)(2,1)S(1)} %bitcast.19), channel_id=1, source_target_pairs={{0,4},{4,0},{1,5},{5,1},{2,6},{6,2},{3,7},{7,3},{8,12},{12,8},{9,1... | collective-permute-start | bytes 589832 | tf_op jit(solution)/shard_map/ppermute | solution.py:247
  104.8 0.9 node_sums.1
  105.8 0.1 collective-permute-done.other_ref
  105.9 0.9 weight_gradients.1
  (16 shorter events, 0.2 us)
Async XLA Ops:
  0.6 0.7 copy-start
  0.6 42.9 %copy-start.3 = (bf16[128,256]{1,0:T(8,128)(2,1)S(1)}, bf16[128,256]{1,0:T(8,128)(2,1)}, u32[]{:S(2)}) copy-start(bf16[128,256]{1,0:T(8,128)(2,1)} %grad_ref.1) | copy-start | bytes 196612
  0.7 42.9 %copy-start.1 = (bf16[256,512]{1,0:T(8,128)(2,1)S(1)}, bf16[256,512]{1,0:T(8,128)(2,1)}, u32[]{:S(2)}) copy-start(bf16[256,512]{1,0:T(8,128)(2,1)} %wkv_ref.1) | copy-start | bytes 786436
  0.7 42.9 %copy-start.2 = (bf16[256,256]{1,0:T(8,128)(2,1)S(1)}, bf16[256,256]{1,0:T(8,128)(2,1)}, u32[]{:S(2)}) copy-start(bf16[256,256]{1,0:T(8,128)(2,1)} %wq_ref.1) | copy-start | bytes 393220
  1.3 0.8 copy-start.4
  2.2 41.4 %copy-start.5 = (s32[128,16]{0,1:T(8,128)S(1)}, s32[128,16]{0,1:T(8,128)}, u32[]{:S(2)}) copy-start(s32[128,16]{0,1:T(8,128)} %param.10) | copy-start | bytes 24580
  100.1 5.8 %collective-permute-start = (bf16[4,8,24,128]{3,2,1,0:T(8,128)(2,1)S(1)}, bf16[4,8,24,128]{3,2,1,0:T(8,128)(2,1)S(1)}, u32[]{:S(2)}, u32[]{:S(2)}) collective-permute-start(bf16[4,8,24,128]{3,2,1,0:T(8,128)(2,1)S(1)} %bitcast.19), channel_id=1, source_target_pairs={{0,4},{4,0},{1,5},{5,1},{2,6},{6,2},{3,7},{7,3},{8,12},{12,8},{9,1... | collective-permute-start | bytes 589832 | tf_op jit(solution)/shard_map/ppermute | solution.py:247

commit v5 on v4

--- a/solution.py
+++ b/solution.py
@@ -60,8 +60,11 @@
     return jnp.concatenate(blocks, 0).T
 
 
-def pick_kernel(rows_ref, node_ref, out_ref, kept_ref):
+def keep_kernel(node_ref, kept_ref):
     kept_ref[...] = node_ref[...]
+
+
+def pick_kernel(rows_ref, node_ref, out_ref):
     nodes = node_ref.shape[0]
     picks = lax.broadcasted_iota(jnp.int32, (nodes, rows_ref.shape[1]), 0) == rows_ref[...]
     picks = jnp.where(picks, 1.0, 0.0).astype(BF16)
@@ -208,21 +211,29 @@
     inner = nz * nc
     owners = ny * inner
 
+    whole = pl.BlockSpec(memory_space=pltpu.VMEM)
+    small = pltpu.CompilerParams(vmem_limit_bytes=SMALL)
+    rows = jax.ShapeDtypeStruct((nodes, features), BF16)
+    kept = pl.pallas_call(
+        keep_kernel,
+        out_shape=rows,
+        in_specs=[whole],
+        out_specs=whole,
+        compiler_params=small,
+        name="keep",
+    )(node_rows)
+    need_rows, kept = lax.optimization_barrier((need_rows, kept))
     wanted = need_rows.reshape(owners, replicas).T
     my_rows = lax.dynamic_index_in_dim(wanted, lax.axis_index("x"), 0, keepdims=False)
     my_rows = my_rows[None, :]
-    whole = pl.BlockSpec(memory_space=pltpu.VMEM)
-    outgoing, kept = pl.pallas_call(
+    outgoing = pl.pallas_call(
         pick_kernel,
-        out_shape=(
-            jax.ShapeDtypeStruct((owners, features), BF16),
-            jax.ShapeDtypeStruct((nodes, features), BF16),
-        ),
+        out_shape=jax.ShapeDtypeStruct((owners, features), BF16),
         in_specs=[whole] * 2,
-        out_specs=(whole,) * 2,
-        compiler_params=pltpu.CompilerParams(vmem_limit_bytes=SMALL),
+        out_specs=whole,
+        compiler_params=small,
         name="pick",
-    )(my_rows, node_rows)
+    )(my_rows, kept)
     incoming = exchange(outgoing.reshape(owners, -1, LANES), ("y", "z", "c")).reshape(owners, features)
     table = lax.all_gather(jnp.concatenate([kept, incoming], 0), "x", axis=0, tiled=True)
 

time: 107 us -> 107 us (level)
  no operation moved by 1% of the time
where the time goes in v5:
time: 107 us; the launch traced here: 106 us
  blocking collectives  93.9 us (88%)
  Pallas kernels  5.41 us (5%)
  starting transfers between devices  4.74 us (4%)
    all_to_all x5, blocking collectives, exchange(): return lax.all_to_all(blocks, axes, split_axis=0, concat_axis=0, tiled=True)  82.5 us
    all_gather x1, blocking collectives, shards(): lax.all_gather(jnp.concatenate([kept, incoming], 0), 'x', axis=0, tiled=T...  11.4 us
    ppermute x1, starting transfers between devices, shards(): other = lax.ppermute(grads, 'c', [(0, 1), (1, 0)])  4.74 us
    pallas_call x1, Pallas kernels, attention(): pl.pallas_call(attention_kernel, out_shape=(jax.ShapeDtypeStruct((nodes,...  3.36 us
  transfers between devices with their start and end apart: 1, of which 1 were waited for; matrix products, arithmetic and copies ran while one was open for 0% of the time, Pallas kernels for 1%

profile of v5, /device:TPU:1, one launch (start us, length us, event | category | flops | bytes accessed | tf_op | source)
XLA Modules:
  0.0 106.3 jit_solution(2151314921435941268)
XLA Ops:
  0.6 0.0 copy-start
  0.6 0.0 copy-start.3
  0.7 0.0 copy-start.1
  0.7 0.0 copy-start.2
  0.7 0.0 copy-start.4
  0.7 0.9 copy-done.4
  1.6 0.0 copy-start.5
  1.6 0.0 copy-done
  1.6 0.2 pick.1
  1.8 29.7 %all_to_all.25 = bf16[128,2,128]{2,1,0:T(2,128)(2,1)S(1)} all-to-all(bf16[128,2,128]{2,1,0:T(2,128)(2,1)S(1)} %reshape.41), channel_id=1, replica_groups=mesh['y'=8,'z'=8,'c'=2,'x'=4] {'y','z','c'}, dimensions={0} | all-to-all | bytes 131072 | tf_op jit(solution)/shard_map/all_to_all | solution.py:33
  31.6 11.4 %all_gather.3.table_ref = bf16[1024,256]{1,0:T(8,128)(2,1)S(1)} all-gather(bf16[256,256]{1,0:T(8,128)(2,1)S(1)} %pad_maximum_fusion.1), channel_id=1, replica_groups=mesh['y'=8,'z'=8,'c'=2,'x'=4] {'x'}, dimensions={0}, use_global_device_ids=true | all-gather | bytes 655360 | tf_op jit(solution)/shard_map/all_gather | solution.py:238
  43.0 0.0 copy-done.3
  43.0 0.0 copy-done.1
  43.0 0.0 copy-done.2
  43.0 0.0 copy-done.5
  43.0 3.4 %attention.1 = (bf16[128,256]{1,0:T(8,128)(2,1)S(1)}, bf16[4,896,128]{2,1,0:T(8,128)(2,1)S(1)}, f32[128,256]{1,0:T(8,128)S(1)}) custom-call(bf16[128,256]{1,0:T(8,128)(2,1)S(1)} %keep.1.node_ref, bf16[128,256]{1,0:T(8,128)(2,1)S(1)} %copy-done.3, s32[16,128]{1,0:T(8,128)S(1)} %bitcast.21, bf16[1024,256]{1,0:T(8,128)(2,1)S(1)} %all_gather.3.table_ref, ...), custom_call_target="tpu_custom_call" | custom-call | tf_op jit(solution)/shard_map/attention/pallas_call | solution.py:193
  46.4 12.1 %all_to_all.26 = bf16[4,896,128]{2,1,0:T(8,128)(2,1)S(1)} all-to-all(bf16[4,896,128]{2,1,0:T(8,128)(2,1)S(1)} %get-tuple-element.15), channel_id=1, replica_groups=mesh['y'=8,'z'=8,'c'=2,'x'=4] {'x'}, dimensions={0} | all-to-all | bytes 1835008 | tf_op jit(solution)/shard_map/all_to_all | solution.py:33
  58.6 0.1 convert_reduce_fusion.summed_ref
  58.8 15.2 %all_to_all.27 = bf16[16,40,128]{2,1,0:T(8,128)(2,1)S(1)} all-to-all(bf16[16,40,128]{2,1,0:T(8,128)(2,1)S(1)} %pad_maximum_fusion), channel_id=1, replica_groups=mesh['y'=8,'z'=8,'c'=2,'x'=4] {'c','z'}, dimensions={0} | all-to-all | bytes 327680 | tf_op jit(solution)/shard_map/all_to_all | solution.py:33
  74.1 10.0 %all_to_all.28.landed_ref = bf16[8,56,128]{2,1,0:T(8,128)(2,1)S(1)} all-to-all(bf16[8,56,128]{2,1,0:T(8,128)(2,1)S(1)} %pad_maximum_fusion.2), channel_id=1, replica_groups=mesh['y'=8,'z'=8,'c'=2,'x'=4] {'y'}, dimensions={0} | all-to-all | bytes 229376 | tf_op jit(solution)/shard_map/all_to_all | solution.py:33
  84.1 15.4 %all_to_all.29 = bf16[32,24,128]{2,1,0:T(8,128)(2,1)S(1)} all-to-all(bf16[32,24,128]{2,1,0:T(8,128)(2,1)S(1)} %broadcast_in_dim.5), channel_id=1, replica_groups=mesh['y'=8,'z'=8,'c'=2,'x'=4] {'x','z'}, dimensions={0} | all-to-all | bytes 393216 | tf_op jit(solution)/shard_map/all_to_all | solution.py:33
  99.5 4.7 %collective-permute-start = (bf16[4,8,24,128]{3,2,1,0:T(8,128)(2,1)S(1)}, bf16[4,8,24,128]{3,2,1,0:T(8,128)(2,1)S(1)}, u32[]{:S(2)}, u32[]{:S(2)}) collective-permute-start(bf16[4,8,24,128]{3,2,1,0:T(8,128)(2,1)S(1)} %bitcast.19), channel_id=1, source_target_pairs={{0,4},{4,0},{1,5},{5,1},{2,6},{6,2},{3,7},{7,3},{8,12},{12,8},{9,1... | collective-permute-start | bytes 589832 | tf_op jit(solution)/shard_map/ppermute | solution.py:258
  104.3 0.9 node_sums.1
  105.2 0.1 collective-permute-done.other_ref
  105.3 0.9 weight_gradients.1
  (17 shorter events, 0.2 us)
Async XLA Ops:
  0.6 1.0 copy-start
  0.6 42.4 %copy-start.3 = (bf16[128,256]{1,0:T(8,128)(2,1)S(1)}, bf16[128,256]{1,0:T(8,128)(2,1)}, u32[]{:S(2)}) copy-start(bf16[128,256]{1,0:T(8,128)(2,1)} %grad_ref.1) | copy-start | bytes 196612
  0.7 42.4 %copy-start.1 = (bf16[256,512]{1,0:T(8,128)(2,1)S(1)}, bf16[256,512]{1,0:T(8,128)(2,1)}, u32[]{:S(2)}) copy-start(bf16[256,512]{1,0:T(8,128)(2,1)} %wkv_ref.1) | copy-start | bytes 786436
  0.7 42.4 %copy-start.2 = (bf16[256,256]{1,0:T(8,128)(2,1)S(1)}, bf16[256,256]{1,0:T(8,128)(2,1)}, u32[]{:S(2)}) copy-start(bf16[256,256]{1,0:T(8,128)(2,1)} %wq_ref.1) | copy-start | bytes 393220
  0.7 0.9 copy-start.4
  1.6 41.5 %copy-start.5 = (s32[128,16]{0,1:T(8,128)S(1)}, s32[128,16]{0,1:T(8,128)}, u32[]{:S(2)}) copy-start(s32[128,16]{0,1:T(8,128)} %param.10) | copy-start | bytes 24580
  99.5 5.8 %collective-permute-start = (bf16[4,8,24,128]{3,2,1,0:T(8,128)(2,1)S(1)}, bf16[4,8,24,128]{3,2,1,0:T(8,128)(2,1)S(1)}, u32[]{:S(2)}, u32[]{:S(2)}) collective-permute-start(bf16[4,8,24,128]{3,2,1,0:T(8,128)(2,1)S(1)} %bitcast.19), channel_id=1, source_target_pairs={{0,4},{4,0},{1,5},{5,1},{2,6},{6,2},{3,7},{7,3},{8,12},{12,8},{9,1... | collective-permute-start | bytes 589832 | tf_op jit(solution)/shard_map/ppermute | solution.py:258

commit v6 on v5

--- a/solution.py
+++ b/solution.py
@@ -127,8 +127,7 @@
 
     keyval = []
     whole_kv = dot(table_ref[...], wkv).astype(BF16)
-    total = jnp.zeros((1, HEADS * nodes), F32)
-    inner = jnp.zeros((1, HEADS * nodes), F32)
+    peaks, totals, inners = [], [], []
     for r in range(replicas):
         span = slice(r * block, (r + 1) * block)
         kv = whole_kv[span, :]
@@ -141,22 +140,29 @@
         count = count.astype(F32)
         log_count = jnp.where(count > 0.0, jnp.log(jnp.maximum(count, 1.0)), -1e30)
         log_count = jnp.concatenate([log_count] * HEADS, 1)
-        weight = jnp.exp(rows_of_both(kv[:, :features], q_scaled) + log_count)
+        score = rows_of_both(kv[:, :features], q_scaled) + log_count
+        peaks.append(jnp.max(score, axis=0, keepdims=True))
+        weight = jnp.exp(score - peaks[r])
         dprob = rows_of_both(kv[:, features:], g_scaled)
-        total = total + jnp.sum(weight, axis=0, keepdims=True)
-        inner = inner + jnp.sum(weight * dprob, axis=0, keepdims=True)
+        totals.append(jnp.sum(weight, axis=0, keepdims=True))
+        inners.append(jnp.sum(weight * dprob, axis=0, keepdims=True))
         weight_scr[span, :] = weight
         dprob_scr[span, :] = dprob
 
-    inverse = 1.0 / total
-    mean = inner * inverse
+    peak = peaks[0]
+    for other in peaks[1:]:
+        peak = jnp.maximum(peak, other)
+    factors = [jnp.exp(part - peak) for part in peaks]
+    inverse = 1.0 / sum(f * t for f, t in zip(factors, totals))
+    factors = [f * inverse for f in factors]
+    mean = sum(f * t for f, t in zip(factors, inners))
     attended = jnp.zeros((features, 2 * nodes), F32)
     dquery = jnp.zeros((features, 2 * nodes), F32)
     all_dkv = []
     for r in range(replicas):
         span = slice(r * block, (r + 1) * block)
         kv = keyval[r]
-        prob = weight_scr[span, :] * inverse
+        prob = weight_scr[span, :] * factors[r]
         dscore = (prob * (dprob_scr[span, :] - mean)).astype(BF16)
         prob = prob.astype(BF16)
         attended = attended + per_pair(kv[:, features:], prob)

time: 107 us -> 107 us (level)
  no operation moved by 1% of the time
where the time goes in v6:
time: 107 us; the launch traced here: 106 us
  blocking collectives  93.9 us (88%)
  Pallas kernels  5.58 us (5%)
  starting transfers between devices  4.74 us (4%)
    all_to_all x5, blocking collectives, exchange(): return lax.all_to_all(blocks, axes, split_axis=0, concat_axis=0, tiled=True)  82.5 us
    all_gather x1, blocking collectives, shards(): lax.all_gather(jnp.concatenate([kept, incoming], 0), 'x', axis=0, tiled=T...  11.4 us
    ppermute x1, starting transfers between devices, shards(): other = lax.ppermute(grads, 'c', [(0, 1), (1, 0)])  4.74 us
    pallas_call x1, Pallas kernels, attention(): pl.pallas_call(attention_kernel, out_shape=(jax.ShapeDtypeStruct((nodes,...  3.53 us
  transfers between devices with their start and end apart: 1, of which 1 were waited for; matrix products, arithmetic and copies ran while one was open for 0% of the time, Pallas kernels for 1%

profile of v6, /device:TPU:1, one launch (start us, length us, event | category | flops | bytes accessed | tf_op | source)
XLA Modules:
  0.0 106.4 jit_solution(5665924304041365427)
XLA Ops:
  0.6 0.0 copy-start
  0.6 0.0 copy-start.3
  0.7 0.0 copy-start.1
  0.7 0.0 copy-start.2
  0.7 0.0 copy-start.4
  0.7 0.9 copy-done.4
  1.6 0.0 copy-start.5
  1.6 0.0 copy-done
  1.6 0.2 pick.1
  1.8 29.7 %all_to_all.25 = bf16[128,2,128]{2,1,0:T(2,128)(2,1)S(1)} all-to-all(bf16[128,2,128]{2,1,0:T(2,128)(2,1)S(1)} %reshape.41), channel_id=1, replica_groups=mesh['y'=8,'z'=8,'c'=2,'x'=4] {'y','z','c'}, dimensions={0} | all-to-all | bytes 131072 | tf_op jit(solution)/shard_map/all_to_all | solution.py:33
  31.6 11.4 %all_gather.3.table_ref = bf16[1024,256]{1,0:T(8,128)(2,1)S(1)} all-gather(bf16[256,256]{1,0:T(8,128)(2,1)S(1)} %pad_maximum_fusion.1), channel_id=1, replica_groups=mesh['y'=8,'z'=8,'c'=2,'x'=4] {'x'}, dimensions={0}, use_global_device_ids=true | all-gather | bytes 655360 | tf_op jit(solution)/shard_map/all_gather | solution.py:244
  43.0 0.0 copy-done.3
  43.0 0.0 copy-done.1
  43.0 0.0 copy-done.2
  43.0 0.0 copy-done.5
  43.0 3.5 %attention.1 = (bf16[128,256]{1,0:T(8,128)(2,1)S(1)}, bf16[4,896,128]{2,1,0:T(8,128)(2,1)S(1)}, f32[128,256]{1,0:T(8,128)S(1)}) custom-call(bf16[128,256]{1,0:T(8,128)(2,1)S(1)} %keep.1.node_ref, bf16[128,256]{1,0:T(8,128)(2,1)S(1)} %copy-done.3, s32[16,128]{1,0:T(8,128)S(1)} %bitcast.21, bf16[1024,256]{1,0:T(8,128)(2,1)S(1)} %all_gather.3.table_ref, ...), custom_call_target="tpu_custom_call" | custom-call | tf_op jit(solution)/shard_map/attention/pallas_call | solution.py:199
  46.6 12.1 %all_to_all.26 = bf16[4,896,128]{2,1,0:T(8,128)(2,1)S(1)} all-to-all(bf16[4,896,128]{2,1,0:T(8,128)(2,1)S(1)} %get-tuple-element.15), channel_id=1, replica_groups=mesh['y'=8,'z'=8,'c'=2,'x'=4] {'x'}, dimensions={0} | all-to-all | bytes 1835008 | tf_op jit(solution)/shard_map/all_to_all | solution.py:33
  58.7 0.1 convert_reduce_fusion.summed_ref
  59.0 15.2 %all_to_all.27 = bf16[16,40,128]{2,1,0:T(8,128)(2,1)S(1)} all-to-all(bf16[16,40,128]{2,1,0:T(8,128)(2,1)S(1)} %pad_maximum_fusion), channel_id=1, replica_groups=mesh['y'=8,'z'=8,'c'=2,'x'=4] {'c','z'}, dimensions={0} | all-to-all | bytes 327680 | tf_op jit(solution)/shard_map/all_to_all | solution.py:33
  74.3 10.0 %all_to_all.28.landed_ref = bf16[8,56,128]{2,1,0:T(8,128)(2,1)S(1)} all-to-all(bf16[8,56,128]{2,1,0:T(8,128)(2,1)S(1)} %pad_maximum_fusion.2), channel_id=1, replica_groups=mesh['y'=8,'z'=8,'c'=2,'x'=4] {'y'}, dimensions={0} | all-to-all | bytes 229376 | tf_op jit(solution)/shard_map/all_to_all | solution.py:33
  84.3 15.4 %all_to_all.29 = bf16[32,24,128]{2,1,0:T(8,128)(2,1)S(1)} all-to-all(bf16[32,24,128]{2,1,0:T(8,128)(2,1)S(1)} %broadcast_in_dim.5), channel_id=1, replica_groups=mesh['y'=8,'z'=8,'c'=2,'x'=4] {'x','z'}, dimensions={0} | all-to-all | bytes 393216 | tf_op jit(solution)/shard_map/all_to_all | solution.py:33
  99.7 4.7 %collective-permute-start = (bf16[4,8,24,128]{3,2,1,0:T(8,128)(2,1)S(1)}, bf16[4,8,24,128]{3,2,1,0:T(8,128)(2,1)S(1)}, u32[]{:S(2)}, u32[]{:S(2)}) collective-permute-start(bf16[4,8,24,128]{3,2,1,0:T(8,128)(2,1)S(1)} %bitcast.19), channel_id=1, source_target_pairs={{0,4},{4,0},{1,5},{5,1},{2,6},{6,2},{3,7},{7,3},{8,12},{12,8},{9,1... | collective-permute-start | bytes 589832 | tf_op jit(solution)/shard_map/ppermute | solution.py:264
  104.5 0.9 node_sums.1
  105.4 0.1 collective-permute-done.other_ref
  105.5 0.9 weight_gradients.1
  (17 shorter events, 0.2 us)
Async XLA Ops:
  0.6 1.0 copy-start
  0.6 42.4 %copy-start.3 = (bf16[128,256]{1,0:T(8,128)(2,1)S(1)}, bf16[128,256]{1,0:T(8,128)(2,1)}, u32[]{:S(2)}) copy-start(bf16[128,256]{1,0:T(8,128)(2,1)} %grad_ref.1) | copy-start | bytes 196612
  0.7 42.4 %copy-start.1 = (bf16[256,512]{1,0:T(8,128)(2,1)S(1)}, bf16[256,512]{1,0:T(8,128)(2,1)}, u32[]{:S(2)}) copy-start(bf16[256,512]{1,0:T(8,128)(2,1)} %wkv_ref.1) | copy-start | bytes 786436
  0.7 42.4 %copy-start.2 = (bf16[256,256]{1,0:T(8,128)(2,1)S(1)}, bf16[256,256]{1,0:T(8,128)(2,1)}, u32[]{:S(2)}) copy-start(bf16[256,256]{1,0:T(8,128)(2,1)} %wq_ref.1) | copy-start | bytes 393220
  0.7 0.9 copy-start.4
  1.6 41.5 %copy-start.5 = (s32[128,16]{0,1:T(8,128)S(1)}, s32[128,16]{0,1:T(8,128)}, u32[]{:S(2)}) copy-start(s32[128,16]{0,1:T(8,128)} %param.10) | copy-start | bytes 24580
  99.7 5.8 %collective-permute-start = (bf16[4,8,24,128]{3,2,1,0:T(8,128)(2,1)S(1)}, bf16[4,8,24,128]{3,2,1,0:T(8,128)(2,1)S(1)}, u32[]{:S(2)}, u32[]{:S(2)}) collective-permute-start(bf16[4,8,24,128]{3,2,1,0:T(8,128)(2,1)S(1)} %bitcast.19), channel_id=1, source_target_pairs={{0,4},{4,0},{1,5},{5,1},{2,6},{6,2},{3,7},{7,3},{8,12},{12,8},{9,1... | collective-permute-start | bytes 589832 | tf_op jit(solution)/shard_map/ppermute | solution.py:264

commit v7 on v6

--- a/solution.py
+++ b/solution.py
@@ -104,26 +104,43 @@
             to_ref[at : at + 8, column : column + LANES] = block[row - first : row - first + 8]
 
 
+def prepare_kernel(node_ref, grad_ref, links_ref, wq_ref, q_ref, g_ref, log_count_ref):
+    nodes = node_ref.shape[0]
+    degree = links_ref.shape[0]
+    replicas = log_count_ref.shape[0] // (2 * nodes)
+    block = 2 * nodes
+    node = node_ref[...]
+    queries = per_head(dot(node, wq_ref[...]).astype(BF16))
+    upstream = per_head(grad_ref[...])
+    q_ref[...], g_ref[...] = queries.astype(BF16), upstream.astype(BF16)
+
+    links = links_ref[...]
+    arrived = links >= replicas * nodes
+    owner = jnp.where(arrived, links - replicas * nodes, links) // nodes
+    links = owner * block + jnp.where(arrived, nodes, 0) + links % nodes
+    for r in range(replicas):
+        here = (lax.broadcasted_iota(jnp.int32, (block, nodes), 0) + r * block).astype(jnp.int16)
+        count = jnp.zeros((block, nodes), BF16)
+        for j in range(degree):
+            hit = here == jnp.broadcast_to(links[j : j + 1, :].astype(jnp.int16), here.shape)
+            count = count + jnp.where(hit, jnp.ones_like(count), jnp.zeros_like(count))
+        count = count.astype(F32)
+        log_count = jnp.where(count > 0.0, jnp.log(jnp.maximum(count, 1.0)), -1e30)
+        log_count_ref[r * block : (r + 1) * block, :] = log_count
+
+
 def attention_kernel(
-    node_ref, grad_ref, links_ref, table_ref, wq_ref, wkv_ref,
+    node_ref, q_ref, g_ref, log_count_ref, table_ref, wq_ref, wkv_ref,
     attended_ref, send_ref, dnode_ref, weight_scr, dprob_scr,
 ):
     nodes, features = node_ref.shape
-    degree = links_ref.shape[0]
     replicas = send_ref.shape[0]
     block = table_ref.shape[0] // replicas
     scale = 1.0 / math.sqrt(HEAD_DIM)
     node = node_ref[...]
     wkv = wkv_ref[...]
-    queries = per_head(dot(node, wq_ref[...]).astype(BF16))
-    upstream = per_head(grad_ref[...])
-    q_heads, q_scaled = queries.astype(BF16), (queries * scale).astype(BF16)
-    g_heads, g_scaled = upstream.astype(BF16), (upstream * scale).astype(BF16)
-
-    links = links_ref[...]
-    arrived = links >= replicas * nodes
-    owner = jnp.where(arrived, links - replicas * nodes, links) // nodes
-    links = owner * block + jnp.where(arrived, nodes, 0) + links % nodes
+    q_heads, g_heads = q_ref[...], g_ref[...]
+    q_scaled, g_scaled = (q_heads * scale).astype(BF16), (g_heads * scale).astype(BF16)
 
     keyval = []
     whole_kv = dot(table_ref[...], wkv).astype(BF16)
@@ -132,13 +149,7 @@
         span = slice(r * block, (r + 1) * block)
         kv = whole_kv[span, :]
         keyval.append(kv)
-        here = (lax.broadcasted_iota(jnp.int32, (block, nodes), 0) + r * block).astype(jnp.int16)
-        count = jnp.zeros((block, nodes), BF16)
-        for j in range(degree):
-            hit = here == jnp.broadcast_to(links[j : j + 1, :].astype(jnp.int16), here.shape)
-            count = count + jnp.where(hit, jnp.ones_like(count), jnp.zeros_like(count))
-        count = count.astype(F32)
-        log_count = jnp.where(count > 0.0, jnp.log(jnp.maximum(count, 1.0)), -1e30)
+        log_count = log_count_ref[span, :]
         log_count = jnp.concatenate([log_count] * HEADS, 1)
         score = rows_of_both(kv[:, :features], q_scaled) + log_count
         peaks.append(jnp.max(score, axis=0, keepdims=True))
@@ -191,7 +202,22 @@
         send_ref[piece // each, at : at + LANES, :] = grads[row : row + LANES, column : column + LANES]
 
 
-def attention(node_rows, grad_out, links, table, w_query, w_keyval, replicas):
+def prepare(node_rows, grad_out, links, w_query, replicas):
+    nodes, features = node_rows.shape
+    whole = pl.BlockSpec(memory_space=pltpu.VMEM)
+    return pl.pallas_call(
+        prepare_kernel,
+        out_shape=(jax.ShapeDtypeStruct((HEADS * nodes, features), BF16),) * 2
+        + (jax.ShapeDtypeStruct((2 * nodes * replicas, nodes), F32),),
+        in_specs=[whole] * 4,
+        out_specs=(whole,) * 3,
+        compiler_params=pltpu.CompilerParams(vmem_limit_bytes=SMALL),
+        cost_estimate=pl.CostEstimate(flops=20000000, bytes_accessed=2000000, transcendentals=130000),
+        name="prepare",
+    )(node_rows, grad_out, links, w_query)
+
+
+def attention(node_rows, q_heads, g_heads, log_count, table, w_query, w_keyval, replicas):
     nodes, features = node_rows.shape
     entries = table.shape[0]
     sent = 4 * nodes + features * (features + w_keyval.shape[1]) // LANES // replicas
@@ -203,12 +229,12 @@
             jax.ShapeDtypeStruct((replicas, sent, LANES), BF16),
             jax.ShapeDtypeStruct((nodes, features), F32),
         ),
-        in_specs=[whole] * 6,
+        in_specs=[whole] * 7,
         out_specs=(whole,) * 3,
         scratch_shapes=[pltpu.VMEM((entries, HEADS * nodes), F32)] * 2,
         compiler_params=pltpu.CompilerParams(vmem_limit_bytes=48 * 1024 * 1024),
         name="attention",
-    )(node_rows, grad_out, links, table, w_query, w_keyval)
+    )(node_rows, q_heads, g_heads, log_count, table, w_query, w_keyval)
 
 
 def shards(node_rows, w_query, w_keyval, need_rows, neighbours, grad_out):
@@ -243,9 +269,8 @@
     incoming = exchange(outgoing.reshape(owners, -1, LANES), ("y", "z", "c")).reshape(owners, features)
     table = lax.all_gather(jnp.concatenate([kept, incoming], 0), "x", axis=0, tiled=True)
 
-    attended, partial, dnode = attention(
-        kept, grad_out, neighbours.T, table, w_query, w_keyval, replicas
-    )
+    ready = prepare(kept, grad_out, neighbours.T, w_query, replicas)
+    attended, partial, dnode = attention(kept, *ready, table, w_query, w_keyval, replicas)
 
     summed = jnp.sum(exchange(partial, "x").astype(F32), 0)
     back = summed[2 * nodes : 4 * nodes].astype(BF16).reshape(2, ny, nz, nc, LANES)

time: 107 us -> 107 us (level)
  blocking collectives: 93.9 us -> 64 us
  starting transfers between devices: 4.74 us -> 23.2 us
  waiting for transfers between devices: 0.11 us -> 8.41 us
  local copies, waits for them, and re-layouts: 1.05 us -> 4.06 us
    all_to_all x5 -> x4, blocking collectives: 82.5 us -> 52.6 us  [exchange(): return lax.all_to_all(blocks, axes, split_axis=0, concat_axis=0, tiled=True)]
    all_to_all x0 -> x1, starting transfers between devices: none -> 18.4 us  [exchange(): return lax.all_to_all(blocks, axes, split_axis=0, concat_axis=0, tiled=True)]
    all_to_all x0 -> x1, waiting for transfers between devices: none -> 8.3 us  [exchange(): return lax.all_to_all(blocks, axes, split_axis=0, concat_axis=0, tiled=True)]
    unnamed x13 -> x15, local copies, waits for them, and re-layouts: 0.92 us -> 3.3 us
  transfers between devices with their start and end apart: 1 -> 2, of which waited for: 1 -> 2; matrix products, arithmetic and copies ran while one was open for 0% -> 0% of each run, Pallas kernels for 1% -> 2%
where the time goes in v7:
time: 107 us
  blocking collectives  64 us (60%)
  starting transfers between devices  23.2 us (22%)
  waiting for transfers between devices  8.41 us (8%)
  Pallas kernels  6.09 us (6%)
  local copies, waits for them, and re-layouts  4.06 us (4%)
    all_to_all x4, blocking collectives, exchange(): return lax.all_to_all(blocks, axes, split_axis=0, concat_axis=0, tiled=True)  52.6 us
    all_to_all x1, starting transfers between devices, exchange(): return lax.all_to_all(blocks, axes, split_axis=0, concat_axis=0, tiled=True)  18.4 us
    all_gather x1, blocking collectives, shards(): lax.all_gather(jnp.concatenate([kept, incoming], 0), 'x', axis=0, tiled=T...  11.4 us
    all_to_all x1, waiting for transfers between devices, exchange(): return lax.all_to_all(blocks, axes, split_axis=0, concat_axis=0, tiled=True)  8.3 us
    ppermute x1, starting transfers between devices, shards(): other = lax.ppermute(grads, 'c', [(0, 1), (1, 0)])  4.74 us
    pallas_call x1, Pallas kernels, attention(): pl.pallas_call(attention_kernel, out_shape=(jax.ShapeDtypeStruct((nodes,...  3.34 us
    unnamed x15, local copies, waits for them, and re-layouts  3.3 us
  transfers between devices with their start and end apart: 2, of which 2 were waited for; matrix products, arithmetic and copies ran while one was open for 0% of the time, Pallas kernels for 2%

profile of v7, /device:TPU:1, one launch (start us, length us, event | category | flops | bytes accessed | tf_op | source)
XLA Modules:
  0.0 106.8 jit_solution(3442616525862925226)
XLA Ops:
  0.6 0.0 copy-start
  0.6 0.0 copy-start.4
  0.7 0.8 copy-done.4
  1.5 0.0 copy-start.2
  1.5 0.0 copy-start.3
  1.5 0.0 copy-done
  1.5 0.2 pick.1
  1.7 0.7 reshape.41
  2.4 18.4 %all-to-all-start = ((bf16[128,2,128]{2,1,0:T(2,128)(2,1)}), bf16[128,2,128]{2,1,0:T(2,128)(2,1)S(1)}, u32[]{:S(2)}, u32[]{:S(2)}) async-start(bf16[128,2,128]{2,1,0:T(2,128)(2,1)} %reshape.41), calls=%async_computation | async-start | bytes 131072 | tf_op jit(solution)/shard_map/all_to_all | solution.py:33
  20.8 0.0 copy-start.1
  20.8 0.9 copy-done.1
  21.7 0.0 copy-start.5
  21.7 0.8 copy-done.5
  22.6 0.0 copy-start.6
  22.6 0.7 copy-done.6
  23.3 0.7 prepare.1
  24.0 8.3 %all-to-all-done = bf16[128,2,128]{2,1,0:T(2,128)(2,1)S(1)} async-done(((bf16[128,2,128]{2,1,0:T(2,128)(2,1)}), bf16[128,2,128]{2,1,0:T(2,128)(2,1)S(1)}, u32[]{:S(2)}, u32[]{:S(2)}) %all-to-all-start) | async-done | bytes 65568 | tf_op jit(solution)/shard_map/all_to_all | solution.py:33
  32.3 11.4 %all_gather.3.table_ref = bf16[1024,256]{1,0:T(8,128)(2,1)S(1)} all-gather(bf16[256,256]{1,0:T(8,128)(2,1)S(1)} %pad_maximum_fusion.1), channel_id=1, replica_groups=mesh['y'=8,'z'=8,'c'=2,'x'=4] {'x'}, dimensions={0}, use_global_device_ids=true | all-gather | bytes 655360 | tf_op jit(solution)/shard_map/all_gather | solution.py:270
  43.7 0.0 copy-done.2
  43.7 0.0 copy-done.3
  43.7 3.3 %attention.1 = (bf16[128,256]{1,0:T(8,128)(2,1)S(1)}, bf16[4,896,128]{2,1,0:T(8,128)(2,1)S(1)}, f32[128,256]{1,0:T(8,128)S(1)}) custom-call(bf16[128,256]{1,0:T(8,128)(2,1)S(1)} %keep.1.node_ref, bf16[512,256]{1,0:T(8,128)(2,1)S(1)} %get-tuple-element.18.q_ref, bf16[512,256]{1,0:T(8,128)(2,1)S(1)} %get-tuple-element.19.g_ref, ...), custom_call_target="tpu_custom_call" | custom-call | tf_op jit(solution)/shard_map/attention/pallas_call | solution.py:225
  47.1 12.1 %all_to_all.25 = bf16[4,896,128]{2,1,0:T(8,128)(2,1)S(1)} all-to-all(bf16[4,896,128]{2,1,0:T(8,128)(2,1)S(1)} %get-tuple-element.21), channel_id=1, replica_groups=mesh['y'=8,'z'=8,'c'=2,'x'=4] {'x'}, dimensions={0} | all-to-all | bytes 1835008 | tf_op jit(solution)/shard_map/all_to_all | solution.py:33
  59.2 0.1 convert_reduce_fusion.summed_ref
  59.5 15.2 %all_to_all.26 = bf16[16,40,128]{2,1,0:T(8,128)(2,1)S(1)} all-to-all(bf16[16,40,128]{2,1,0:T(8,128)(2,1)S(1)} %pad_maximum_fusion), channel_id=1, replica_groups=mesh['y'=8,'z'=8,'c'=2,'x'=4] {'c','z'}, dimensions={0} | all-to-all | bytes 327680 | tf_op jit(solution)/shard_map/all_to_all | solution.py:33
  74.7 10.2 %all_to_all.27.landed_ref = bf16[8,56,128]{2,1,0:T(8,128)(2,1)S(1)} all-to-all(bf16[8,56,128]{2,1,0:T(8,128)(2,1)S(1)} %pad_maximum_fusion.2), channel_id=1, replica_groups=mesh['y'=8,'z'=8,'c'=2,'x'=4] {'y'}, dimensions={0} | all-to-all | bytes 229376 | tf_op jit(solution)/shard_map/all_to_all | solution.py:33
  85.0 15.1 %all_to_all.28 = bf16[32,24,128]{2,1,0:T(8,128)(2,1)S(1)} all-to-all(bf16[32,24,128]{2,1,0:T(8,128)(2,1)S(1)} %broadcast_in_dim.5), channel_id=1, replica_groups=mesh['y'=8,'z'=8,'c'=2,'x'=4] {'x','z'}, dimensions={0} | all-to-all | bytes 393216 | tf_op jit(solution)/shard_map/all_to_all | solution.py:33
  100.1 4.7 %collective-permute-start = (bf16[4,8,24,128]{3,2,1,0:T(8,128)(2,1)S(1)}, bf16[4,8,24,128]{3,2,1,0:T(8,128)(2,1)S(1)}, u32[]{:S(2)}, u32[]{:S(2)}) collective-permute-start(bf16[4,8,24,128]{3,2,1,0:T(8,128)(2,1)S(1)} %bitcast.19), channel_id=1, source_target_pairs={{0,4},{4,0},{1,5},{5,1},{2,6},{6,2},{3,7},{7,3},{8,12},{12,8},{9,1... | collective-permute-start | bytes 589832 | tf_op jit(solution)/shard_map/ppermute | solution.py:289
  104.9 0.9 node_sums.1
  105.8 0.1 collective-permute-done.other_ref
  105.9 0.9 weight_gradients.1
  (16 shorter events, 0.2 us)
Async XLA Ops:
  0.6 0.9 copy-start
  0.6 0.8 copy-start.4
  1.5 42.2 %copy-start.2 = (bf16[256,256]{1,0:T(8,128)(2,1)S(1)}, bf16[256,256]{1,0:T(8,128)(2,1)}, u32[]{:S(2)}) copy-start(bf16[256,256]{1,0:T(8,128)(2,1)} %wq_ref.3) | copy-start | bytes 393220
  1.5 42.2 %copy-start.3 = (bf16[256,512]{1,0:T(8,128)(2,1)S(1)}, bf16[256,512]{1,0:T(8,128)(2,1)}, u32[]{:S(2)}) copy-start(bf16[256,512]{1,0:T(8,128)(2,1)} %wkv_ref.1) | copy-start | bytes 786436
  2.4 29.9 %all-to-all-start = ((bf16[128,2,128]{2,1,0:T(2,128)(2,1)}), bf16[128,2,128]{2,1,0:T(2,128)(2,1)S(1)}, u32[]{:S(2)}, u32[]{:S(2)}) async-start(bf16[128,2,128]{2,1,0:T(2,128)(2,1)} %reshape.41), calls=%async_computation | async-start | bytes 131072 | tf_op jit(solution)/shard_map/all_to_all | solution.py:33
  20.8 0.9 copy-start.1
  21.7 0.8 copy-start.5
  22.6 0.7 copy-start.6
  100.1 5.8 %collective-permute-start = (bf16[4,8,24,128]{3,2,1,0:T(8,128)(2,1)S(1)}, bf16[4,8,24,128]{3,2,1,0:T(8,128)(2,1)S(1)}, u32[]{:S(2)}, u32[]{:S(2)}) collective-permute-start(bf16[4,8,24,128]{3,2,1,0:T(8,128)(2,1)S(1)} %bitcast.19), channel_id=1, source_target_pairs={{0,4},{4,0},{1,5},{5,1},{2,6},{6,2},{3,7},{7,3},{8,12},{12,8},{9,1... | collective-permute-start | bytes 589832 | tf_op jit(solution)/shard_map/ppermute | solution.py:289

commit v8 on v6

--- a/solution.py
+++ b/solution.py
@@ -138,7 +138,7 @@
             hit = here == jnp.broadcast_to(links[j : j + 1, :].astype(jnp.int16), here.shape)
             count = count + jnp.where(hit, jnp.ones_like(count), jnp.zeros_like(count))
         count = count.astype(F32)
-        log_count = jnp.where(count > 0.0, jnp.log(jnp.maximum(count, 1.0)), -1e30)
+        log_count = jnp.maximum(jnp.log(count), -1e30)
         log_count = jnp.concatenate([log_count] * HEADS, 1)
         score = rows_of_both(kv[:, :features], q_scaled) + log_count
         peaks.append(jnp.max(score, axis=0, keepdims=True))

time: 107 us -> 107 us (level)
  no operation moved by 1% of the time
where the time goes in v8:
time: 107 us; the launch traced here: 106 us
  blocking collectives  93.9 us (88%)
  Pallas kernels  5.53 us (5%)
  starting transfers between devices  4.74 us (4%)
    all_to_all x5, blocking collectives, exchange(): return lax.all_to_all(blocks, axes, split_axis=0, concat_axis=0, tiled=True)  82.5 us
    all_gather x1, blocking collectives, shards(): lax.all_gather(jnp.concatenate([kept, incoming], 0), 'x', axis=0, tiled=T...  11.4 us
    ppermute x1, starting transfers between devices, shards(): other = lax.ppermute(grads, 'c', [(0, 1), (1, 0)])  4.74 us
    pallas_call x1, Pallas kernels, attention(): pl.pallas_call(attention_kernel, out_shape=(jax.ShapeDtypeStruct((nodes,...  3.48 us
  transfers between devices with their start and end apart: 1, of which 1 were waited for; matrix products, arithmetic and copies ran while one was open for 0% of the time, Pallas kernels for 1%

profile of v8, /device:TPU:1, one launch (start us, length us, event | category | flops | bytes accessed | tf_op | source)
XLA Modules:
  0.0 106.4 jit_solution(16370412352406714931)
XLA Ops:
  0.6 0.0 copy-start
  0.6 0.0 copy-start.3
  0.7 0.0 copy-start.1
  0.7 0.0 copy-start.2
  0.7 0.0 copy-start.4
  0.7 0.9 copy-done.4
  1.6 0.0 copy-start.5
  1.6 0.0 copy-done
  1.6 0.2 pick.1
  1.8 29.7 %all_to_all.25 = bf16[128,2,128]{2,1,0:T(2,128)(2,1)S(1)} all-to-all(bf16[128,2,128]{2,1,0:T(2,128)(2,1)S(1)} %reshape.41), channel_id=1, replica_groups=mesh['y'=8,'z'=8,'c'=2,'x'=4] {'y','z','c'}, dimensions={0} | all-to-all | bytes 131072 | tf_op jit(solution)/shard_map/all_to_all | solution.py:33
  31.6 11.4 %all_gather.3.table_ref = bf16[1024,256]{1,0:T(8,128)(2,1)S(1)} all-gather(bf16[256,256]{1,0:T(8,128)(2,1)S(1)} %pad_maximum_fusion.1), channel_id=1, replica_groups=mesh['y'=8,'z'=8,'c'=2,'x'=4] {'x'}, dimensions={0}, use_global_device_ids=true | all-gather | bytes 655360 | tf_op jit(solution)/shard_map/all_gather | solution.py:244
  43.0 0.0 copy-done.3
  43.0 0.0 copy-done.1
  43.0 0.0 copy-done.2
  43.0 0.0 copy-done.5
  43.0 3.5 %attention.1 = (bf16[128,256]{1,0:T(8,128)(2,1)S(1)}, bf16[4,896,128]{2,1,0:T(8,128)(2,1)S(1)}, f32[128,256]{1,0:T(8,128)S(1)}) custom-call(bf16[128,256]{1,0:T(8,128)(2,1)S(1)} %keep.1.node_ref, bf16[128,256]{1,0:T(8,128)(2,1)S(1)} %copy-done.3, s32[16,128]{1,0:T(8,128)S(1)} %bitcast.21, bf16[1024,256]{1,0:T(8,128)(2,1)S(1)} %all_gather.3.table_ref, ...), custom_call_target="tpu_custom_call" | custom-call | tf_op jit(solution)/shard_map/attention/pallas_call | solution.py:199
  46.5 12.1 %all_to_all.26 = bf16[4,896,128]{2,1,0:T(8,128)(2,1)S(1)} all-to-all(bf16[4,896,128]{2,1,0:T(8,128)(2,1)S(1)} %get-tuple-element.15), channel_id=1, replica_groups=mesh['y'=8,'z'=8,'c'=2,'x'=4] {'x'}, dimensions={0} | all-to-all | bytes 1835008 | tf_op jit(solution)/shard_map/all_to_all | solution.py:33
  58.7 0.1 convert_reduce_fusion.summed_ref
  58.9 15.2 %all_to_all.27 = bf16[16,40,128]{2,1,0:T(8,128)(2,1)S(1)} all-to-all(bf16[16,40,128]{2,1,0:T(8,128)(2,1)S(1)} %pad_maximum_fusion), channel_id=1, replica_groups=mesh['y'=8,'z'=8,'c'=2,'x'=4] {'c','z'}, dimensions={0} | all-to-all | bytes 327680 | tf_op jit(solution)/shard_map/all_to_all | solution.py:33
  74.2 10.0 %all_to_all.28.landed_ref = bf16[8,56,128]{2,1,0:T(8,128)(2,1)S(1)} all-to-all(bf16[8,56,128]{2,1,0:T(8,128)(2,1)S(1)} %pad_maximum_fusion.2), channel_id=1, replica_groups=mesh['y'=8,'z'=8,'c'=2,'x'=4] {'y'}, dimensions={0} | all-to-all | bytes 229376 | tf_op jit(solution)/shard_map/all_to_all | solution.py:33
  84.2 15.4 %all_to_all.29 = bf16[32,24,128]{2,1,0:T(8,128)(2,1)S(1)} all-to-all(bf16[32,24,128]{2,1,0:T(8,128)(2,1)S(1)} %broadcast_in_dim.5), channel_id=1, replica_groups=mesh['y'=8,'z'=8,'c'=2,'x'=4] {'x','z'}, dimensions={0} | all-to-all | bytes 393216 | tf_op jit(solution)/shard_map/all_to_all | solution.py:33
  99.6 4.7 %collective-permute-start = (bf16[4,8,24,128]{3,2,1,0:T(8,128)(2,1)S(1)}, bf16[4,8,24,128]{3,2,1,0:T(8,128)(2,1)S(1)}, u32[]{:S(2)}, u32[]{:S(2)}) collective-permute-start(bf16[4,8,24,128]{3,2,1,0:T(8,128)(2,1)S(1)} %bitcast.19), channel_id=1, source_target_pairs={{0,4},{4,0},{1,5},{5,1},{2,6},{6,2},{3,7},{7,3},{8,12},{12,8},{9,1... | collective-permute-start | bytes 589832 | tf_op jit(solution)/shard_map/ppermute | solution.py:264
  104.4 0.9 node_sums.1
  105.3 0.1 collective-permute-done.other_ref
  105.5 0.9 weight_gradients.1
  (17 shorter events, 0.2 us)
Async XLA Ops:
  0.6 1.0 copy-start
  0.6 42.4 %copy-start.3 = (bf16[128,256]{1,0:T(8,128)(2,1)S(1)}, bf16[128,256]{1,0:T(8,128)(2,1)}, u32[]{:S(2)}) copy-start(bf16[128,256]{1,0:T(8,128)(2,1)} %grad_ref.1) | copy-start | bytes 196612
  0.7 42.4 %copy-start.1 = (bf16[256,512]{1,0:T(8,128)(2,1)S(1)}, bf16[256,512]{1,0:T(8,128)(2,1)}, u32[]{:S(2)}) copy-start(bf16[256,512]{1,0:T(8,128)(2,1)} %wkv_ref.1) | copy-start | bytes 786436
  0.7 42.4 %copy-start.2 = (bf16[256,256]{1,0:T(8,128)(2,1)S(1)}, bf16[256,256]{1,0:T(8,128)(2,1)}, u32[]{:S(2)}) copy-start(bf16[256,256]{1,0:T(8,128)(2,1)} %wq_ref.1) | copy-start | bytes 393220
  0.7 0.9 copy-start.4
  1.6 41.5 %copy-start.5 = (s32[128,16]{0,1:T(8,128)S(1)}, s32[128,16]{0,1:T(8,128)}, u32[]{:S(2)}) copy-start(s32[128,16]{0,1:T(8,128)} %param.10) | copy-start | bytes 24580
  99.6 5.8 %collective-permute-start = (bf16[4,8,24,128]{3,2,1,0:T(8,128)(2,1)S(1)}, bf16[4,8,24,128]{3,2,1,0:T(8,128)(2,1)S(1)}, u32[]{:S(2)}, u32[]{:S(2)}) collective-permute-start(bf16[4,8,24,128]{3,2,1,0:T(8,128)(2,1)S(1)} %bitcast.19), channel_id=1, source_target_pairs={{0,4},{4,0},{1,5},{5,1},{2,6},{6,2},{3,7},{7,3},{8,12},{12,8},{9,1... | collective-permute-start | bytes 589832 | tf_op jit(solution)/shard_map/ppermute | solution.py:264
